TPU v7x, 256 devices: a whole 4x4x8 slice. The times are simulated.
256 devices in a mesh: lon: 16 (over x, y_lo, core), lat: 16 (over z, y_hi).
Axes of the slice: x: 4, y: 4 (y_hi: 2, y_lo: 2; y = y_hi * 2 + y_lo), z: 8, core: 2. Of those that a mesh axis runs over, the one named last changes fastest.
Arguments:
- field: float32 [256, 256, 768], P('lat', 'lon'), may hold values from -6 to 6
- w_qkv: bfloat16 [2, 768, 2304], replicated, may hold values from -2 to 2
- w_proj: bfloat16 [2, 768, 768], replicated, may hold values from -0.21875 to 0.21875
- norm_gain: float32 [2, 768], replicated, may hold values from 0.1 to 1.9
- pos_bias: float32 [2, 12, 64, 64], replicated, may hold values from -4 to 4
Outputs:
- blended: float32 [256, 256, 768], P('lat', 'lon')
All inputs are finite; a program needn't handle non-finite values.
Results may differ from a plain program's by a relative error of at most 0.0055.
Values may be sent and summed in bfloat16 or wider, within the bound.
A program may use at most 64 MiB of HBM per device.

v0:
```python
import jax
import jax.numpy as jnp
from jax import lax
from jax.sharding import PartitionSpec as P

HEADS = 12
WINDOW = 8
SHIFT = 4
WIN_TOKENS = 64


def shifted(block, axis, distance):
    devices = range(lax.axis_size(axis))
    route = [((i - distance) % len(devices), i) for i in devices]
    return lax.ppermute(block, axis, route)


def shortened(value):

    def short(part):
        return part.astype(jnp.bfloat16) if part.dtype == jnp.float32 else part

    return jax.tree.map(short, value)


def layer_norm(x, gain):
    mean = jnp.mean(x, axis=-1, keepdims=True)
    centred = x - mean
    var = jnp.mean(centred * centred, axis=-1, keepdims=True)
    return centred * lax.rsqrt(var + 1e-05) * gain


def to_windows(x):
    height, span, depth = x.shape
    grid = x.reshape(height // WINDOW, WINDOW, span // WINDOW, WINDOW, depth).transpose(
        0, 2, 1, 3, 4
    )
    return grid.reshape(-1, WIN_TOKENS, depth)


def from_windows(y, height, span):
    depth = y.shape[-1]
    grid = y.reshape(height // WINDOW, span // WINDOW, WINDOW, WINDOW, depth).transpose(
        0, 2, 1, 3, 4
    )
    return grid.reshape(height, span, depth)


def window_attention(query, keys, values, bias, allowed):
    count = query.shape[0]
    head_dim = query.shape[-1]
    scores = jnp.einsum("wqhd,wkhd->whqk", query, keys, preferred_element_type=jnp.float32)
    scores = scores * head_dim ** (-0.5) + bias[None]
    scores = jnp.where(allowed[:, None], scores, -1e30)
    top = jnp.max(scores, axis=-1, keepdims=True)
    expo = jnp.exp(scores - top)
    probs = (expo / jnp.sum(expo, axis=-1, keepdims=True)).astype(jnp.bfloat16)
    context = jnp.einsum("whqk,wkhd->wqhd", probs, values, preferred_element_type=jnp.float32)
    return context.astype(jnp.bfloat16).reshape(count, WIN_TOKENS, -1)


def project_qkv(normed, weight):
    width = weight.shape[0]
    flat = normed.reshape(-1, width)
    return jnp.dot(flat, weight, preferred_element_type=jnp.float32).astype(jnp.bfloat16)


def on_device(field, w_qkv, w_proj, norm_gain, pos_bias):
    rows, cols, width = field.shape
    head_dim = width // HEADS
    wins = to_windows(field)
    count = wins.shape[0]
    normed = layer_norm(wins, norm_gain[0]).astype(jnp.bfloat16)
    qkv = project_qkv(normed, w_qkv[0]).reshape(count, WIN_TOKENS, 3, HEADS, head_dim)
    everyone = jnp.ones((count, WIN_TOKENS, WIN_TOKENS), dtype=bool)
    context = window_attention(qkv[:, :, 0], qkv[:, :, 1], qkv[:, :, 2], pos_bias[0], everyone)
    update = jnp.dot(context.reshape(-1, width), w_proj[0], preferred_element_type=jnp.float32)
    state = from_windows(wins + update.reshape(wins.shape), rows, cols)
    lat_index = lax.axis_index("lat")
    total_lat = rows * lax.axis_size("lat")
    arrived = shifted(state[:SHIFT], "lat", -1)
    moved = jnp.concatenate([state[SHIFT:], arrived], axis=0)
    arrived_cols = shifted(moved[:, :SHIFT], "lon", -1)
    moved = jnp.concatenate([moved[:, SHIFT:], arrived_cols], axis=1)
    lat_rows = (lat_index * rows + SHIFT + jnp.arange(rows, dtype=jnp.int32)) % total_lat
    groups = (lat_rows + SHIFT) // WINDOW
    group_grid = jnp.broadcast_to(groups[:, None, None], (rows, cols, 1))
    group_wins = to_windows(group_grid)[..., 0]
    allowed = group_wins[:, :, None] == group_wins[:, None, :]
    wins = to_windows(moved)
    normed = layer_norm(wins, norm_gain[1]).astype(jnp.bfloat16)
    qkv = project_qkv(normed, w_qkv[1]).reshape(count, WIN_TOKENS, 3, HEADS, head_dim)
    context = window_attention(qkv[:, :, 0], qkv[:, :, 1], qkv[:, :, 2], pos_bias[1], allowed)
    update = jnp.dot(context.reshape(-1, width), w_proj[1], preferred_element_type=jnp.float32)
    result = from_windows(wins + update.reshape(wins.shape), rows, cols)
    returned_cols = shifted(result[:, cols - SHIFT :].astype(jnp.bfloat16), "lon", 1).astype(
        jnp.float32
    )
    result = jnp.concatenate([returned_cols, result[:, : cols - SHIFT]], axis=1)
    returned_rows = shifted(shortened(result[rows - SHIFT :]), "lat", 1)
    result = jnp.concatenate([returned_rows, result[: rows - SHIFT]], axis=0)
    return result


def solution(mesh):
    return jax.shard_map(
        on_device,
        mesh=mesh,
        in_specs=(P("lat", "lon", None), P(), P(), P(), P()),
        out_specs=P("lat", "lon", None),
        check_vma=False,
    )
```

profile of v0, /device:TPU:0, one launch (start us, length us, event | category | flops | bytes accessed | tf_op | source)
XLA Modules:
  0.0 74.0 jit_solution(5147784811135647309)
XLA Ops:
  0.0 1.3 %bitcast_reduce_fusion = f32[2,2,8,8]{3,2,1,0:T(8,128)S(1)} fusion(f32[2,8,2,8,768]{4,3,2,1,0:T(8,128)} %bitcast.85), kind=kLoop, calls=%fused_computation.36 | loop fusion | flops 196352 | bytes 787456 | tf_op jit(solution)/shard_map/reduce_sum | solution.py:27
  1.3 2.1 %copy.82 = f32[2,8,2,8,768]{4,3,1,2,0:T(8,128)} copy(f32[2,8,2,8,768]{4,3,2,1,0:T(8,128)} %bitcast.86) | data formatting | bytes 1572864 | tf_op jit(solution)/shard_map/reshape | solution.py:35
  3.9 3.1 %convolution_convert_fusion.1 = bf16[256,2304]{1,0:T(8,128)(2,1)S(1)} fusion(bf16[256,768]{1,0:T(8,128)(2,1)S(1)} %bitcast.101, bf16[2,768,2304]{2,1,0:T(8,128)(2,1)} %param.6), kind=kOutput, calls=%fused_computation.3 | convolution fusion | flops 906559488 | bytes 5111808 | tf_op jit(solution)/shard_map/dot_general | solution.py:65
  7.0 0.6 copy.83
  7.6 1.0 %reshape.168 = bf16[4,64,3,12,64]{1,0,4,3,2:T(4,128)(2,1)S(1)} reshape(bf16[256,2304]{0,1:T(8,128)(2,1)S(1)} %copy.83) | data formatting | bytes 2359296 | tf_op jit(solution)/shard_map/reshape | solution.py:74
  8.6 2.3 %fusion.31 = (bf16[4,64,1,12,64]{1,0,4,3,2:T(4,128)(2,1)}, bf16[4,64,1,12,64]{1,0,4,3,2:T(4,128)(2,1)}, bf16[4,64,1,12,64]{1,0,4,3,2:T(4,128)(2,1)S(1)}) fusion(bf16[4,64,3,12,64]{1,0,4,3,2:T(4,128)(2,1)S(1)} %reshape.168), kind=kLoop, calls=%fused_computation.71 | loop fusion | bytes 2359296 | tf_op jit(solution)/shard_map/slice | solution.py:76
  10.9 1.5 %copy.110 = bf16[4,64,1,12,64]{4,1,3,0,2:T(8,128)(2,1)S(1)} copy(bf16[4,64,1,12,64]{1,0,4,3,2:T(4,128)(2,1)} %get-tuple-element.10) | data formatting | bytes 786432
  12.4 0.6 copy.111
  13.1 1.2 %slice_bitcast_fusion = (f32[12,64,64]{2,1,0:T(8,128)S(1)}, f32[12,64,64]{2,1,0:T(8,128)S(1)}) fusion(f32[2,12,64,64]{3,2,1,0:T(8,128)} %param.9), kind=kLoop, calls=%fused_computation.44 | loop fusion | bytes 786432 | tf_op jit(solution)/shard_map/add | solution.py:53
  15.0 1.1 %fusion.32 = f32[4,12,64]{2,1,0:T(8,128)} fusion(f32[4,12,64,64]{2,3,1,0:T(8,128)S(1)} %multiply_add_fusion), kind=kOutput, calls=%fused_computation.72 | output fusion | flops 393279 | bytes 798720 | tf_op jit(solution)/shard_map/sub | solution.py:56
  16.1 3.7 %convolution_convert_fusion.3 = bf16[4,12,64,64]{3,2,1,0:T(8,128)(2,1)} fusion(bf16[4,64,1,12,64]{1,0,4,3,2:T(4,128)(2,1)} %get-tuple-element.11, f32[4,12,64]{2,1,0:T(8,128)} %fusion.32, f32[4,12,64,64]{2,3,1,0:T(8,128)} %copy-done.6), kind=kOutput, calls=%fused_computation.17 | convolution fusion | flops 25955392 | bytes 1585152 | tf_op jit(solution)/shard_map/whqk,wkhd->wqhd/dot_general | solution.py:58
  19.9 1.7 %convolution_add_fusion = f32[4,64,768]{2,1,0:T(8,128)S(1)} fusion(f32[4,64,768]{2,1,0:T(8,128)S(1)} %bitcast.92, bf16[4,64,768]{1,2,0:T(8,128)(2,1)} %bitcast.98, bf16[2,768,768]{2,1,0:T(8,128)(2,1)S(1)} %copy-done.3), kind=kOutput, calls=%fused_computation.18 | convolution fusion | flops 302186496 | bytes 3145728 | tf_op jit(solution)/shard_map/dot_general | solution.py:77
  21.7 6.8 %collective-permute-start = (f32[4,16,768]{2,1,0:T(8,128)S(1)}, f32[4,16,768]{2,1,0:T(8,128)S(1)}, u32[]{:S(2)}, u32[]{:S(2)}) collective-permute-start(f32[4,16,768]{2,1,0:T(8,128)S(1)} %slice.94), channel_id=1, source_target_pairs={{1,0},{2,1},{3,2},{4,3},{5,4},{6,5},{7,6},{8,7},{9,8},{10,9},{11,1... | collective-permute-start | bytes 589832 | tf_op jit(solution)/shard_map/ppermute | solution.py:15
  28.7 3.9 %collective-permute-done = f32[4,16,768]{2,1,0:T(8,128)S(1)} collective-permute-done((f32[4,16,768]{2,1,0:T(8,128)S(1)}, f32[4,16,768]{2,1,0:T(8,128)S(1)}, u32[]{:S(2)}, u32[]{:S(2)}) %collective-permute-start) | collective-permute-done | bytes 196640 | tf_op jit(solution)/shard_map/ppermute | solution.py:15
  32.7 1.7 %collective-permute-start.1 = (f32[16,4,768]{2,1,0:T(4,128)S(1)}, f32[16,4,768]{2,1,0:T(4,128)S(1)}, u32[]{:S(2)}, u32[]{:S(2)}) collective-permute-start(f32[16,4,768]{2,1,0:T(4,128)S(1)} %pad_maximum_fusion.2), channel_id=1, source_target_pairs={{16,0},{32,16},{48,32},{64,48},{80,64},{96,80},{112,96},{128,112},... | collective-permute-start | bytes 589832 | tf_op jit(solution)/shard_map/ppermute | solution.py:15
  34.4 0.7 broadcast_compare_fusion
  35.1 0.9 %copy.101 = f32[12,64,64]{1,2,0:T(8,128)} copy(f32[12,64,64]{2,1,0:T(8,128)S(1)} %get-tuple-element.13) | data formatting | bytes 393216 | tf_op jit(solution)/shard_map/add | solution.py:53
  36.1 1.5 %collective-permute-done.1 = f32[16,4,768]{2,1,0:T(4,128)S(1)} collective-permute-done((f32[16,4,768]{2,1,0:T(4,128)S(1)}, f32[16,4,768]{2,1,0:T(4,128)S(1)}, u32[]{:S(2)}, u32[]{:S(2)}) %collective-permute-start.1) | collective-permute-done | bytes 196640 | tf_op jit(solution)/shard_map/ppermute | solution.py:15
  37.6 0.9 %copy.91 = f32[2,2,8,8,768]{4,3,2,1,0:T(8,128)} copy(f32[2,2,8,8,768]{4,3,1,2,0:T(8,128)S(1)} %bitcast.81) | data formatting | bytes 1572864 | tf_op jit(solution)/shard_map/transpose | solution.py:35
  39.2 3.1 %convolution_convert_fusion = bf16[256,2304]{1,0:T(8,128)(2,1)S(1)} fusion(bf16[256,768]{1,0:T(8,128)(2,1)S(1)} %bitcast.100, bf16[2,768,2304]{2,1,0:T(8,128)(2,1)} %param.6), kind=kOutput, calls=%fused_computation.2 | convolution fusion | flops 906559488 | bytes 5111808 | tf_op jit(solution)/shard_map/dot_general | solution.py:65
  42.3 0.6 copy.97
  43.0 1.0 %reshape.173 = bf16[4,64,3,12,64]{1,0,4,3,2:T(4,128)(2,1)S(1)} reshape(bf16[256,2304]{0,1:T(8,128)(2,1)S(1)} %copy.97) | data formatting | bytes 2359296 | tf_op jit(solution)/shard_map/reshape | solution.py:92
  44.0 2.3 %fusion.30 = (bf16[4,64,1,12,64]{1,0,4,3,2:T(4,128)(2,1)}, bf16[4,64,1,12,64]{1,0,4,3,2:T(4,128)(2,1)}, bf16[4,64,1,12,64]{1,0,4,3,2:T(4,128)(2,1)S(1)}) fusion(bf16[4,64,3,12,64]{1,0,4,3,2:T(4,128)(2,1)S(1)} %reshape.173), kind=kLoop, calls=%fused_computation.70 | loop fusion | bytes 2359296 | tf_op jit(solution)/shard_map/slice | solution.py:93
  46.3 1.6 %copy.113 = bf16[4,64,1,12,64]{4,1,3,0,2:T(8,128)(2,1)S(1)} copy(bf16[4,64,1,12,64]{1,0,4,3,2:T(4,128)(2,1)} %get-tuple-element.7) | data formatting | bytes 786432
  47.9 0.6 copy.114
  49.5 0.7 copy-done.5
  50.2 0.6 copy-done.8
  50.8 3.5 %convolution_convert_fusion.2 = bf16[4,12,64,64]{3,2,1,0:T(8,128)(2,1)} fusion(bf16[4,64,1,12,64]{1,0,4,3,2:T(4,128)(2,1)S(1)} %copy-done.8, f32[4,12,64]{2,1,0:T(8,128)S(1)} %fusion.33, f32[4,12,64,64]{2,3,1,0:T(8,128)} %copy-done.5), kind=kOutput, calls=%fused_computation.16 | convolution fusion | flops 25955392 | bytes 1585152 | tf_op jit(solution)/shard_map/whqk,wkhd->wqhd/dot_general | solution.py:58
  54.3 1.7 %fusion.10 = f32[4,64,768]{2,1,0:T(8,128)S(1)} fusion(bf16[4,64,768]{1,2,0:T(8,128)(2,1)} %bitcast.99, bf16[2,768,768]{2,1,0:T(8,128)(2,1)S(1)} %copy-done.4), kind=kOutput, calls=%fused_computation.19 | convolution fusion | flops 301989888 | bytes 2359296 | tf_op jit(solution)/shard_map/dot_general | solution.py:94
  56.3 6.4 %collective-permute-done.2 = bf16[16,4,768]{2,1,0:T(4,128)(2,1)S(1)} collective-permute-done((bf16[16,4,768]{2,1,0:T(4,128)(2,1)S(1)}, bf16[16,4,768]{2,1,0:T(4,128)(2,1)S(1)}, u32[]{:S(2)}, u32[]{:S(2)}) %collective-permute-start.2) | collective-permute-done | bytes 98336 | tf_op jit(solution)/shard_map/ppermute | solution.py:15
  63.0 10.0 %collective-permute-done.3 = bf16[4,16,768]{2,1,0:T(8,128)(2,1)S(1)} collective-permute-done((bf16[4,16,768]{2,1,0:T(8,128)(2,1)S(1)}, bf16[4,16,768]{2,1,0:T(8,128)(2,1)S(1)}, u32[]{:S(2)}, u32[]{:S(2)}) %collective-permute-start.3) | collective-permute-done | bytes 98336 | tf_op jit(solution)/shard_map/ppermute | solution.py:15
  73.0 1.0 %fusion.15 = f32[16,16,768]{2,1,0:T(8,128)} fusion(f32[16,12,768]{2,1,0:T(8,128)S(1)} %bitcast.91, f32[16,4,768]{2,1,0:T(4,128)S(1)} %convert_element_type.58, f32[4,16,768]{2,1,0:T(8,128)S(1)} %convert_element_type.59), kind=kLoop, calls=%fused_computation.25 | loop fusion | flops 393216 | bytes 1769472 | tf_op jit(solution)/shard_map/concatenate | solution.py:101
  (54 shorter events, 3.7 us)
Async XLA Ops:
  0.0 3.4 %copy-start = (f32[16,16,768]{2,1,0:T(8,128)S(1)}, f32[16,16,768]{2,1,0:T(8,128)}, u32[]{:S(2)}) copy-start(f32[16,16,768]{2,1,0:T(8,128)} %param.5) | copy-start | bytes 2359300
  0.0 3.7 %copy-start.10 = (f32[2,768]{1,0:T(2,128)S(1)}, f32[2,768]{1,0:T(2,128)}, u32[]{:S(2)}) copy-start(f32[2,768]{1,0:T(2,128)} %param.8) | copy-start | bytes 18436
  15.0 1.2 %copy-start.6 = (f32[4,12,64,64]{2,3,1,0:T(8,128)}, f32[4,12,64,64]{2,3,1,0:T(8,128)S(1)}, u32[]{:S(2)}) copy-start(f32[4,12,64,64]{2,3,1,0:T(8,128)S(1)} %multiply_add_fusion) | copy-start | bytes 2359300
  16.1 3.8 %copy-start.1 = (f32[2,8,2,8,768]{4,3,1,2,0:T(8,128)S(1)}, f32[2,8,2,8,768]{4,3,1,2,0:T(8,128)}, u32[]{:S(2)}) copy-start(f32[2,8,2,8,768]{4,3,1,2,0:T(8,128)} %copy.82) | copy-start | bytes 2359300
  16.1 3.8 %copy-start.3 = (bf16[2,768,768]{2,1,0:T(8,128)(2,1)S(1)}, bf16[2,768,768]{2,1,0:T(8,128)(2,1)}, u32[]{:S(2)}) copy-start(bf16[2,768,768]{2,1,0:T(8,128)(2,1)} %param.7) | copy-start | bytes 7077892
  21.7 11.0 %collective-permute-start = (f32[4,16,768]{2,1,0:T(8,128)S(1)}, f32[4,16,768]{2,1,0:T(8,128)S(1)}, u32[]{:S(2)}, u32[]{:S(2)}) collective-permute-start(f32[4,16,768]{2,1,0:T(8,128)S(1)} %slice.94), channel_id=1, source_target_pairs={{1,0},{2,1},{3,2},{4,3},{5,4},{6,5},{7,6},{8,7},{9,8},{10,9},{11,1... | collective-permute-start | bytes 589832 | tf_op jit(solution)/shard_map/ppermute | solution.py:15
  32.7 4.9 %collective-permute-start.1 = (f32[16,4,768]{2,1,0:T(4,128)S(1)}, f32[16,4,768]{2,1,0:T(4,128)S(1)}, u32[]{:S(2)}, u32[]{:S(2)}) collective-permute-start(f32[16,4,768]{2,1,0:T(4,128)S(1)} %pad_maximum_fusion.2), channel_id=1, source_target_pairs={{16,0},{32,16},{48,32},{64,48},{80,64},{96,80},{112,96},{128,112},... | collective-permute-start | bytes 589832 | tf_op jit(solution)/shard_map/ppermute | solution.py:15
  46.3 2.2 %copy-start.7 = (f32[12,64,64]{1,2,0:T(8,128)S(1)}, f32[12,64,64]{1,2,0:T(8,128)}, u32[]{:S(2)}) copy-start(f32[12,64,64]{1,2,0:T(8,128)} %copy.101) | copy-start | bytes 589828
  46.3 2.3 %copy-start.9 = (pred[4,64,64]{1,2,0:T(8,128)(4,1)S(1)}, pred[4,64,64]{1,2,0:T(8,128)(4,1)}, u32[]{:S(2)}) copy-start(pred[4,64,64]{1,2,0:T(8,128)(4,1)} %broadcast_compare_fusion) | copy-start | bytes 49156
  49.1 1.2 %copy-start.5 = (f32[4,12,64,64]{2,3,1,0:T(8,128)}, f32[4,12,64,64]{2,3,1,0:T(8,128)S(1)}, u32[]{:S(2)}) copy-start(f32[4,12,64,64]{2,3,1,0:T(8,128)S(1)} %add_select_fusion) | copy-start | bytes 2359300
  49.1 1.7 %copy-start.8 = (bf16[4,64,1,12,64]{1,0,4,3,2:T(4,128)(2,1)S(1)}, bf16[4,64,1,12,64]{1,0,4,3,2:T(4,128)(2,1)}, u32[]{:S(2)}) copy-start(bf16[4,64,1,12,64]{1,0,4,3,2:T(4,128)(2,1)} %get-tuple-element.8) | copy-start | bytes 1179652
  50.8 3.5 %copy-start.4 = (bf16[2,768,768]{2,1,0:T(8,128)(2,1)S(1)}, bf16[2,768,768]{2,1,0:T(8,128)(2,1)}, u32[]{:S(2)}) copy-start(bf16[2,768,768]{2,1,0:T(8,128)(2,1)} %param.7) | copy-start | bytes 7077892
  54.3 1.8 %copy-start.2 = (f32[2,2,8,8,768]{4,3,2,1,0:T(8,128)S(1)}, f32[2,2,8,8,768]{4,3,2,1,0:T(8,128)}, u32[]{:S(2)}) copy-start(f32[2,2,8,8,768]{4,3,2,1,0:T(8,128)} %copy.91) | copy-start | bytes 2359300
  56.3 6.5 %collective-permute-start.2 = (bf16[16,4,768]{2,1,0:T(4,128)(2,1)S(1)}, bf16[16,4,768]{2,1,0:T(4,128)(2,1)S(1)}, u32[]{:S(2)}, u32[]{:S(2)}) collective-permute-start(bf16[16,4,768]{2,1,0:T(4,128)(2,1)S(1)} %slice.135), channel_id=1, source_target_pairs={{240,0},{0,16},{16,32},{32,48},{48,64},{64,80},{80,96},{96,112},{1... | collective-permute-start | bytes 294920 | tf_op jit(solution)/shard_map/ppermute | solution.py:15
  62.8 10.2 %collective-permute-start.3 = (bf16[4,16,768]{2,1,0:T(8,128)(2,1)S(1)}, bf16[4,16,768]{2,1,0:T(8,128)(2,1)S(1)}, u32[]{:S(2)}, u32[]{:S(2)}) collective-permute-start(bf16[4,16,768]{2,1,0:T(8,128)(2,1)S(1)} %fusion.23), channel_id=1, source_target_pairs={{15,0},{0,1},{1,2},{2,3},{3,4},{4,5},{5,6},{6,7},{7,8},{8,9},{9,10... | collective-permute-start | bytes 294920 | tf_op jit(solution)/shard_map/ppermute | solution.py:15
where the time goes:
time: 74.4 us; the launch traced here: 74 us
  waiting for transfers between devices  21.9 us (29%)
  local copies, waits for them, and re-layouts  19.3 us (26%)
  matrix products  17.9 us (24%)
  starting transfers between devices  8.78 us (12%)
  other arithmetic  5.83 us (8%)
    ppermute x4, waiting for transfers between devices, shifted(): return lax.ppermute(block, axis, route)  21.9 us
    ppermute x4, starting transfers between devices, shifted(): return lax.ppermute(block, axis, route)  8.78 us
    dot_general x2, matrix products, window_attention(): jnp.einsum('whqk,wkhd->wqhd', probs, values, preferred_element_type=jnp.f...  7.23 us
    dot_general x2, matrix products, project_qkv(): jnp.dot(flat, weight, preferred_element_type=jnp.float32)  6.21 us
    unnamed x26, local copies, waits for them, and re-layouts  5.74 us
    slice x2, local copies, waits for them, and re-layouts, on_device(): qkv[:, :, 0]  4.55 us
    add x3, local copies, waits for them, and re-layouts, window_attention(): scores = scores * head_dim ** (-0.5) + bias[None]  2.24 us
    reshape x1, local copies, waits for them, and re-layouts, to_windows(): x.reshape(height // WINDOW, WINDOW, span // WINDOW, WINDOW, depth)  2.08 us
  transfers between devices with their start and end apart: 4, of which 4 were waited for; matrix products, arithmetic and copies ran while one was open for 3% of the time, Pallas kernels for 0%

commit v1 on v0

v1 whole, which is shorter than its diff:
```python
import functools

import jax
import jax.numpy as jnp
from jax import lax
from jax.experimental import pallas as pl
from jax.experimental.pallas import tpu as pltpu
from jax.sharding import PartitionSpec as P

D = 768
HEADS = 12
PAIRS = HEADS // 2
WIN = 64
QUAD = 16
F32 = jnp.float32
BF16 = jnp.bfloat16
MESH = pl.DeviceIdType.MESH
NT = (((1,), (1,)), ((), ()))

ROUTES = ((-1, 0), (1, 0), (0, -1), (0, 1), (-1, -1), (-1, 1), (1, -1), (1, 1))


def route_slices(step):
    if step == -1:
        return pl.ds(1, 1), pl.ds(5, 1)
    if step == 1:
        return pl.ds(4, 1), pl.ds(0, 1)
    return pl.ds(1, 4), pl.ds(1, 4)


def layer_norm(x, gain):
    mean = jnp.mean(x, axis=-1, keepdims=True)
    centred = x - mean
    var = jnp.mean(centred * centred, axis=-1, keepdims=True)
    return centred * lax.rsqrt(var + 1e-05) * gain


def lanes_low(shape, axis):
    return lax.broadcasted_iota(jnp.int32, shape, axis) < 64


def attend(qs, ks, vs, biases):
    low = lanes_low((1, 128), 1)
    keep0 = low.astype(F32).astype(BF16)
    keep1 = (1.0 - low.astype(F32)).astype(BF16)
    diag = (lanes_low((128, 128), 0) == lanes_low((128, 128), 1)).astype(F32).astype(BF16)
    scores = []
    for q, k, bias in zip(qs, ks, biases):
        both = jnp.concatenate([k * keep0, k * keep1], axis=0)
        scores.append(lax.dot_general(q, both, NT, preferred_element_type=F32) + bias)
    tops = []
    for s in scores:
        top0 = jnp.max(jnp.where(low, s, -jnp.inf), axis=-1, keepdims=True)
        top1 = jnp.max(jnp.where(low, -jnp.inf, s), axis=-1, keepdims=True)
        tops.append(jnp.where(low, top0, top1))
    expos = [jnp.exp(s - top).astype(BF16) for s, top in zip(scores, tops)]
    outs = []
    for e, v in zip(expos, vs):
        both = jnp.concatenate([v * keep0, v * keep1], axis=0)
        both = jnp.concatenate([both, diag], axis=1)
        o = jnp.dot(e, both, preferred_element_type=F32)
        outs.append((o[:, :128] / o[:, 128:]).astype(BF16))
    return outs


def natural_of_quad(shape, axis):
    n = lax.broadcasted_iota(jnp.int32, shape, axis)
    u, v, r, c = (n >> 5) & 1, (n >> 4) & 1, (n >> 2) & 3, n & 3
    return (u * 4 + r) * 8 + v * 4 + c


def kernel(
    field, w_qkv, w_proj, gains, pos_bias, out,
    x, wqkv, wproj, gain, bias, bias0, bias1, normed, qkv, ctx, ext, q1, kv1, ctxq,
    load_sem, out_sem, send_sem, recv_sem,
):
    lat, lon = lax.axis_index("lat"), lax.axis_index("lon")
    n_lat, n_lon = lax.axis_size("lat"), lax.axis_size("lon")

    def partner(dy, dx):
        there = {"lat": lax.rem(lat + dy + n_lat, n_lat), "lon": lax.rem(lon + dx + n_lon, n_lon)}
        return there

    barrier = pltpu.get_barrier_semaphore()
    for dy, dx in ROUTES:
        pl.semaphore_signal(barrier, inc=1, device_id=partner(dy, dx), device_id_type=MESH)

    loads = []

    def load(src, dst):
        copy = pltpu.make_async_copy(src, dst, load_sem.at[len(loads)])
        loads.append(copy)
        return copy

    ld_x = load(field, x)
    ld_gain = load(gains, gain)
    ld_qkv = [
        [load(w_qkv.at[s, :, pl.ds(D * c, D)], wqkv.at[s, :, pl.ds(D * c, D)]) for c in range(3)]
        for s in range(2)
    ]
    ld_bias = [load(pos_bias.at[s], bias.at[s]) for s in range(2)]
    ld_proj = [load(w_proj.at[s], wproj.at[s]) for s in range(2)]
    for copy in [ld_x, ld_gain, *ld_qkv[0], ld_bias[0], ld_proj[0]]:
        copy.start()

    ld_x.wait()
    ld_gain.wait()
    windows = [(i, j) for i in range(2) for j in range(2)]
    for w, (i, j) in enumerate(windows):
        cells = x[8 * i:8 * i + 8, 8 * j:8 * j + 8, :].reshape(WIN, D)
        normed[WIN * w:WIN * w + WIN, :] = layer_norm(cells, gain[0:1, :]).astype(BF16)
    for copy in [*ld_qkv[1], ld_bias[1], ld_proj[1]]:
        copy.start()
    for c in range(3):
        ld_qkv[0][c].wait()
        part = jnp.dot(normed[...], wqkv[0, :, D * c:D * c + D], preferred_element_type=F32)
        if c == 0:
            part = part * 0.125
        qkv[:, D * c:D * c + D] = part.astype(BF16)
    ld_bias[0].wait()
    for p in range(PAIRS):
        bias0[p] = jnp.concatenate([bias[0, 2 * p], bias[0, 2 * p + 1]], axis=1)
    for w in range(4):
        rows = slice(WIN * w, WIN * w + WIN)
        cols = [slice(128 * p, 128 * p + 128) for p in range(PAIRS)]
        outs = attend(
            [qkv[rows, 128 * p:128 * p + 128] for p in range(PAIRS)],
            [qkv[rows, D + 128 * p:D + 128 * p + 128] for p in range(PAIRS)],
            [qkv[rows, 2 * D + 128 * p:2 * D + 128 * p + 128] for p in range(PAIRS)],
            [bias0[p] for p in range(PAIRS)],
        )
        for p in range(PAIRS):
            ctx[rows, cols[p]] = outs[p]
    ld_proj[0].wait()
    update = jnp.dot(ctx[...], wproj[0], preferred_element_type=F32)

    quad_rows = (
        natural_of_quad((WIN, WIN), 0) == lax.broadcasted_iota(jnp.int32, (WIN, WIN), 1)
    ).astype(F32)
    nat_rows = (
        natural_of_quad((WIN, WIN), 1) == lax.broadcasted_iota(jnp.int32, (WIN, WIN), 0)
    ).astype(F32)
    for w, (i, j) in enumerate(windows):
        cells = x[8 * i:8 * i + 8, 8 * j:8 * j + 8, :].reshape(WIN, D)
        cells = cells + update[WIN * w:WIN * w + WIN, :]
        x[8 * i:8 * i + 8, 8 * j:8 * j + 8, :] = cells.reshape(8, 8, D)
        unit = layer_norm(cells, gain[1:2, :]).astype(BF16)
        unit = jnp.dot(quad_rows.astype(BF16), unit, preferred_element_type=F32).astype(BF16)
        ext[1 + 2 * i:3 + 2 * i, 1 + 2 * j:3 + 2 * j] = unit.reshape(2, 2, QUAD, D)

    pl.semaphore_wait(barrier, len(ROUTES))
    sends = []
    for n, (dy, dx) in enumerate(ROUTES):
        (src_r, dst_r), (src_c, dst_c) = route_slices(dy), route_slices(dx)
        copy = pltpu.make_async_remote_copy(
            src_ref=ext.at[src_r, src_c],
            dst_ref=ext.at[dst_r, dst_c],
            send_sem=send_sem.at[n],
            recv_sem=recv_sem.at[n],
            device_id=partner(dy, dx),
            device_id_type=MESH,
        )
        copy.start()
        sends.append(copy)

    for copy in ld_qkv[1]:
        copy.wait()
    own = ext[1:5, 1:5].reshape(256, D)
    own_q = jnp.dot(own, wqkv[1, :, :D], preferred_element_type=F32) * 0.125
    q1[...] = own_q.astype(BF16).reshape(4, 4, QUAD, D)
    own_kv = jnp.dot(own, wqkv[1, :, D:], preferred_element_type=F32)
    kv1[1:5, 1:5] = own_kv.astype(BF16).reshape(4, 4, QUAD, 2 * D)
    ld_bias[1].wait()
    twice = jnp.concatenate(
        [
            jnp.concatenate([nat_rows, jnp.zeros_like(nat_rows)], axis=1),
            jnp.concatenate([jnp.zeros_like(nat_rows), nat_rows], axis=1),
        ],
        axis=0,
    )
    for p in range(PAIRS):
        b = jnp.concatenate([bias[1, 2 * p], bias[1, 2 * p + 1]], axis=1)
        b = jnp.dot(quad_rows, b, precision=lax.Precision.HIGHEST, preferred_element_type=F32)
        b = jnp.dot(b, twice, precision=lax.Precision.HIGHEST, preferred_element_type=F32)
        bias1[p] = b.reshape(2, 2, QUAD, 128)

    lane = lax.broadcasted_iota(jnp.int32, (1, 128), 1)
    north = (lane & 63) < 32
    closed_n = jnp.where(lat == 0, -1e30, 0.0)
    closed_s = jnp.where(lat == n_lat - 1, -1e30, 0.0)

    def shifted(a, b):
        r0, r1 = max(2 * a - 1, 0), min(2 * a, 3) + 1
        c0, c1 = max(2 * b - 1, 0), min(2 * b, 3) + 1
        u0, v0 = r0 - (2 * a - 1), c0 - (2 * b - 1)
        nr, nc = r1 - r0, c1 - c0
        count = nr * nc * QUAD
        biases = []
        for p in range(PAIRS):
            part = bias1[p, u0:u0 + nr, v0:v0 + nc].reshape(count, 128)
            if a == 0:
                part = part + jnp.where(north, closed_n, 0.0)
            if a == 2:
                part = part + jnp.where(north, 0.0, closed_s)
            biases.append(part)
        here = (slice(2 * a, 2 * a + 2), slice(2 * b, 2 * b + 2), slice(None))
        outs = attend(
            [q1[r0:r1, c0:c1, :, 128 * p:128 * p + 128].reshape(count, 128) for p in range(PAIRS)],
            [kv1[(*here, slice(128 * p, 128 * p + 128))].reshape(WIN, 128) for p in range(PAIRS)],
            [kv1[(*here, slice(D + 128 * p, D + 128 * p + 128))].reshape(WIN, 128) for p in range(PAIRS)],
            biases,
        )
        for p in range(PAIRS):
            ctxq[r0:r1, c0:c1, :, 128 * p:128 * p + 128] = outs[p].reshape(nr, nc, QUAD, 128)

    shifted(1, 1)

    def halo_kv(units):
        return jnp.dot(units, wqkv[1, :, D:], preferred_element_type=F32).astype(BF16)

    sends[2].wait_recv()
    sends[3].wait_recv()
    units = jnp.concatenate([ext[1:5, 0].reshape(64, D), ext[1:5, 5].reshape(64, D)], axis=0)
    got = halo_kv(units)
    kv1[1:5, 0] = got[:64].reshape(4, QUAD, 2 * D)
    kv1[1:5, 5] = got[64:].reshape(4, QUAD, 2 * D)
    shifted(1, 0)
    shifted(1, 2)
    for n in (0, 1, 4, 5, 6, 7):
        sends[n].wait_recv()
    units = jnp.concatenate([ext[0].reshape(96, D), ext[5].reshape(96, D)], axis=0)
    got = halo_kv(units)
    kv1[0] = got[:96].reshape(6, QUAD, 2 * D)
    kv1[5] = got[96:].reshape(6, QUAD, 2 * D)
    for b in range(3):
        shifted(0, b)
        shifted(2, b)

    for w, (i, j) in enumerate(windows):
        block = ctxq[2 * i:2 * i + 2, 2 * j:2 * j + 2].reshape(WIN, D)
        block = jnp.dot(nat_rows.astype(BF16), block, preferred_element_type=F32)
        ctx[WIN * w:WIN * w + WIN, :] = block.astype(BF16)
    ld_proj[1].wait()
    update = jnp.dot(ctx[...], wproj[1], preferred_element_type=F32)
    for w, (i, j) in enumerate(windows):
        cells = x[8 * i:8 * i + 8, 8 * j:8 * j + 8, :].reshape(WIN, D)
        cells = cells + update[WIN * w:WIN * w + WIN, :]
        x[8 * i:8 * i + 8, 8 * j:8 * j + 8, :] = cells.reshape(8, 8, D)
    store = pltpu.make_async_copy(x, out, out_sem)
    store.start()
    for copy in sends:
        copy.wait_send()
    store.wait()


def on_device(field, w_qkv, w_proj, norm_gain, pos_bias):
    rows, cols, width = field.shape
    any_space = pl.BlockSpec(memory_space=pl.ANY)
    vmem = pltpu.VMEM
    return pl.pallas_call(
        kernel,
        out_shape=jax.ShapeDtypeStruct(field.shape, F32),
        in_specs=[any_space] * 5,
        out_specs=any_space,
        scratch_shapes=[
            vmem((rows, cols, D), F32),
            vmem((2, D, 3 * D), BF16),
            vmem((2, D, D), BF16),
            vmem((2, D), F32),
            vmem((2, HEADS, WIN, WIN), F32),
            vmem((PAIRS, WIN, 128), F32),
            vmem((PAIRS, 2, 2, QUAD, 128), F32),
            vmem((256, D), BF16),
            vmem((256, 3 * D), BF16),
            vmem((256, D), BF16),
            vmem((6, 6, QUAD, D), BF16),
            vmem((4, 4, QUAD, D), BF16),
            vmem((6, 6, QUAD, 2 * D), BF16),
            vmem((4, 4, QUAD, D), BF16),
            pltpu.SemaphoreType.DMA((12,)),
            pltpu.SemaphoreType.DMA,
            pltpu.SemaphoreType.DMA((len(ROUTES),)),
            pltpu.SemaphoreType.DMA((len(ROUTES),)),
        ],
        compiler_params=pltpu.CompilerParams(
            collective_id=0, has_side_effects=True, vmem_limit_bytes=48 * 1024 * 1024
        ),
        cost_estimate=pl.CostEstimate(
            flops=3_300_000_000, bytes_accessed=13_000_000, transcendentals=400_000
        ),
        name="swin_pair",
    )(field, w_qkv, w_proj, norm_gain, pos_bias)


def solution(mesh):
    return jax.shard_map(
        on_device,
        mesh=mesh,
        in_specs=(P("lat", "lon", None), P(), P(), P(), P()),
        out_specs=P("lat", "lon", None),
        check_vma=False,
    )
```

time: 74.4 us -> 28.3 us (0.38)
  the two profiles are of different devices: /device:TPU:0 before, /device:TPU:1 now
where the time goes in v1:
time: 28.3 us; the launch traced here: 28.1 us
  Pallas kernels  22.6 us (80%)
  local copies, waits for them, and re-layouts  5.5 us (19%)
    pallas_call x1, Pallas kernels, on_device(): pl.pallas_call(kernel, out_shape=jax.ShapeDtypeStruct(field.shape, F32),...  22.6 us
    unnamed x9, local copies, waits for them, and re-layouts  5.5 us

profile of v1, /device:TPU:1, one launch (start us, length us, event | category | flops | bytes accessed | tf_op | source)
XLA Modules:
  0.0 28.1 jit_solution(13208545697369475598)
XLA Ops:
  0.0 0.0 copy-start
  0.0 1.7 %copy-done = bf16[2,768,768]{2,1,0:T(8,128)(2,1)S(1)} copy-done((bf16[2,768,768]{2,1,0:T(8,128)(2,1)S(1)}, bf16[2,768,768]{2,1,0:T(8,128)(2,1)}, u32[]{:S(2)}) %copy-start) | copy-done | bytes 2359320
  1.7 0.0 copy-start.1
  1.7 1.1 %copy-done.1 = f32[16,16,768]{2,1,0:T(8,128)S(1)} copy-done((f32[16,16,768]{2,1,0:T(8,128)S(1)}, f32[16,16,768]{2,1,0:T(8,128)}, u32[]{:S(2)}) %copy-start.1) | copy-done | bytes 786456
  2.8 0.0 copy-start.2
  2.8 1.1 %copy-done.2 = f32[2,12,64,64]{3,2,1,0:T(8,128)S(1)} copy-done((f32[2,12,64,64]{3,2,1,0:T(8,128)S(1)}, f32[2,12,64,64]{3,2,1,0:T(8,128)}, u32[]{:S(2)}) %copy-start.2) | copy-done | bytes 393240
  3.9 0.0 copy-start.3
  3.9 0.7 %copy-done.3 = f32[2,768]{1,0:T(2,128)S(1)} copy-done((f32[2,768]{1,0:T(2,128)S(1)}, f32[2,768]{1,0:T(2,128)}, u32[]{:S(2)}) %copy-start.3) | copy-done | bytes 6168
  4.6 22.6 %swin_pair.1 = f32[16,16,768]{2,1,0:T(8,128)S(1)} custom-call(f32[16,16,768]{2,1,0:T(8,128)S(1)} %copy-done.1, bf16[2,768,2304]{2,1,0:T(8,128)(2,1)} %w_qkv.1, bf16[2,768,768]{2,1,0:T(8,128)(2,1)S(1)} %copy-done, f32[2,768]{1,0:T(2,128)S(1)} %copy-done.3, f32[2,12,64,64]{3,2,1,0:T(8,128)S(1)} %copy-done.2), custom_call_target="tpu_custom_call" | custom-call | flops 3300000000 | bytes 13000000 | tf_op jit(solution)/shard_map/swin_pair/pallas_call | solution.py:260
  27.2 0.9 %copy.7 = f32[16,16,768]{2,1,0:T(8,128)} copy(f32[16,16,768]{2,1,0:T(8,128)S(1)} %swin_pair.1) | data formatting | bytes 1572864
Async XLA Ops:
  0.0 1.7 %copy-start = (bf16[2,768,768]{2,1,0:T(8,128)(2,1)S(1)}, bf16[2,768,768]{2,1,0:T(8,128)(2,1)}, u32[]{:S(2)}) copy-start(bf16[2,768,768]{2,1,0:T(8,128)(2,1)} %w_proj.1) | copy-start | bytes 7077892
  1.7 1.1 %copy-start.1 = (f32[16,16,768]{2,1,0:T(8,128)S(1)}, f32[16,16,768]{2,1,0:T(8,128)}, u32[]{:S(2)}) copy-start(f32[16,16,768]{2,1,0:T(8,128)} %field.1) | copy-start | bytes 2359300
  2.8 1.1 %copy-start.2 = (f32[2,12,64,64]{3,2,1,0:T(8,128)S(1)}, f32[2,12,64,64]{3,2,1,0:T(8,128)}, u32[]{:S(2)}) copy-start(f32[2,12,64,64]{3,2,1,0:T(8,128)} %pos_bias.1) | copy-start | bytes 1179652
  3.9 0.7 %copy-start.3 = (f32[2,768]{1,0:T(2,128)S(1)}, f32[2,768]{1,0:T(2,128)}, u32[]{:S(2)}) copy-start(f32[2,768]{1,0:T(2,128)} %gains.1) | copy-start | bytes 18436

commit v2 on v1

v2 whole, which is shorter than its diff:
```python
import functools

import jax
import jax.numpy as jnp
from jax import lax
from jax.experimental import pallas as pl
from jax.experimental.pallas import tpu as pltpu
from jax.sharding import PartitionSpec as P

D = 768
HEADS = 12
PAIRS = HEADS // 2
WIN = 64
QUAD = 16
F32 = jnp.float32
BF16 = jnp.bfloat16
MESH = pl.DeviceIdType.MESH
NT = (((1,), (1,)), ((), ()))

PEERS = ((-1, 0), (1, 0), (0, -1), (0, 1), (-1, -1), (-1, 1), (1, -1), (1, 1))
OWN = slice(1, 5)


def piece(dy, dx, rows=OWN):
    def axis(step, run):
        if step == 0:
            return pl.ds(run.start, run.stop - run.start), pl.ds(run.start, run.stop - run.start)
        return (pl.ds(1, 1), pl.ds(5, 1)) if step < 0 else (pl.ds(4, 1), pl.ds(0, 1))

    (src_r, dst_r), (src_c, dst_c) = axis(dy, rows), axis(dx, OWN)
    return dy, dx, (src_r, src_c), (dst_r, dst_c)


WAVES = tuple(
    (
        piece(dy, 0), piece(dy, -1), piece(dy, 1),
        piece(0, -1, slice(top, top + 2)), piece(0, 1, slice(top, top + 2)),
    )
    for dy, top in ((-1, 1), (1, 3))
)


def layer_norm(x, gain):
    mean = jnp.mean(x, axis=-1, keepdims=True)
    centred = x - mean
    var = jnp.mean(centred * centred, axis=-1, keepdims=True)
    return centred * lax.rsqrt(var + 1e-05) * gain


def lanes_low(shape, axis):
    return lax.broadcasted_iota(jnp.int32, shape, axis) < 64


def attend(qs, ks, vs, biases):
    low = lanes_low((1, 128), 1)
    keep0 = low.astype(F32).astype(BF16)
    keep1 = (1.0 - low.astype(F32)).astype(BF16)
    diag = (lanes_low((128, 128), 0) == lanes_low((128, 128), 1)).astype(F32).astype(BF16)
    scores = []
    for q, k, bias in zip(qs, ks, biases):
        both = jnp.concatenate([k * keep0, k * keep1], axis=0)
        scores.append(lax.dot_general(q, both, NT, preferred_element_type=F32) + bias)
    tops = []
    for s in scores:
        top0 = jnp.max(jnp.where(low, s, -jnp.inf), axis=-1, keepdims=True)
        top1 = jnp.max(jnp.where(low, -jnp.inf, s), axis=-1, keepdims=True)
        tops.append(jnp.where(low, top0, top1))
    expos = [jnp.exp(s - top).astype(BF16) for s, top in zip(scores, tops)]
    outs = []
    for e, v in zip(expos, vs):
        both = jnp.concatenate([v * keep0, v * keep1], axis=0)
        both = jnp.concatenate([both, diag], axis=1)
        o = jnp.dot(e, both, preferred_element_type=F32)
        outs.append((o[:, :128] / o[:, 128:]).astype(BF16))
    return outs


def halves(width):
    return lax.broadcasted_iota(jnp.int32, (1, 8, width), 1) < 4


def to_quads(cells):
    n, _, width = cells.shape
    pairs = cells.reshape(n // 2, 2, 8, width)
    even, odd = pairs[:, 0], pairs[:, 1]
    left = jnp.where(halves(width), even, pltpu.roll(odd, 4, 1))
    right = jnp.where(halves(width), pltpu.roll(even, 4, 1), odd)
    return left, right


def from_quads(left, right):
    n, _, width = left.shape
    even = jnp.where(halves(width), left, pltpu.roll(right, 4, 1))
    odd = jnp.where(halves(width), pltpu.roll(left, 4, 1), right)
    return jnp.stack([even, odd], axis=1).reshape(2 * n, 8, width)


def window_quads(cells):
    width = cells.shape[-1]
    left, right = to_quads(cells)
    both = [side.reshape(2, QUAD, width) for side in (left, right)]
    return jnp.stack(both, axis=1)


def natural_of_quad(shape, axis):
    n = lax.broadcasted_iota(jnp.int32, shape, axis)
    u, v, r, c = (n >> 5) & 1, (n >> 4) & 1, (n >> 2) & 3, n & 3
    return (u * 4 + r) * 8 + v * 4 + c


def kernel(
    field, w_qkv, w_proj, gains, pos_bias, out,
    x, xq, wqkv, wproj, gain, bias, bias0, bias1, normed, nquad, q0, kv0, ext, q1, kv1, ctx,
    load_sem, out_sem, send_sem, recv_sem,
):
    lat, lon = lax.axis_index("lat"), lax.axis_index("lon")
    n_lat, n_lon = lax.axis_size("lat"), lax.axis_size("lon")

    def partner(dy, dx):
        return {"lat": lax.rem(lat + dy + n_lat, n_lat), "lon": lax.rem(lon + dx + n_lon, n_lon)}

    def where_inside(dy, act):
        if dy == 0:
            act()
        else:
            pl.when(lat > 0 if dy < 0 else lat < n_lat - 1)(act)

    barrier = pltpu.get_barrier_semaphore()
    for dy, dx in PEERS:
        where_inside(dy, lambda: pl.semaphore_signal(
            barrier, inc=1, device_id=partner(dy, dx), device_id_type=MESH))

    loads = []

    def load(src, dst):
        copy = pltpu.make_async_copy(src, dst, load_sem.at[len(loads)])
        loads.append(copy)
        return copy

    ld_x = load(field, x)
    ld_gain = load(gains, gain)
    ld_qkv = [
        [load(w_qkv.at[s, :, pl.ds(D * c, D)], wqkv.at[s, :, pl.ds(D * c, D)]) for c in range(3)]
        for s in range(2)
    ]
    ld_bias = [load(pos_bias.at[s], bias.at[s]) for s in range(2)]
    ld_proj = [load(w_proj.at[s], wproj.at[s]) for s in range(2)]
    for copy in [ld_x, ld_gain, *ld_qkv[0], ld_bias[0], ld_proj[0]]:
        copy.start()

    ld_x.wait()
    ld_gain.wait()
    for i in range(2):
        for j in range(2):
            w = 2 * i + j
            quads = (slice(2 * i, 2 * i + 2), slice(2 * j, 2 * j + 2))
            cells = x[8 * i:8 * i + 8, 8 * j:8 * j + 8, :]
            unit = layer_norm(cells, gain[0:1, :])
            normed[WIN * w:WIN * w + WIN, :] = unit.reshape(WIN, D).astype(BF16)
            nquad[quads] = window_quads(unit).astype(BF16)
            xq[quads] = window_quads(cells)
    ld_qkv[0][0].wait()
    part = jnp.dot(nquad[...].reshape(256, D), wqkv[0, :, :D], preferred_element_type=F32) * 0.125
    q0[...] = part.astype(BF16).reshape(4, 4, QUAD, D)
    for c in range(2):
        ld_qkv[0][1 + c].wait()
        part = jnp.dot(
            normed[...], wqkv[0, :, D + D * c:2 * D + D * c], preferred_element_type=F32
        )
        kv0[:, D * c:D * c + D] = part.astype(BF16)
    ld_bias[0].wait()

    def pair_bias(s, p):
        b = jnp.concatenate([bias[s, 2 * p], bias[s, 2 * p + 1]], axis=1)
        return window_quads(b.reshape(8, 8, 128)).reshape(WIN, 128)

    for p in range(PAIRS):
        bias0[p] = pair_bias(0, p)
    ld_proj[0].wait()
    for copy in [*ld_qkv[1], ld_bias[1], ld_proj[1]]:
        copy.start()

    sends = []

    def send(n, dy, dx, src, dst):
        copy = pltpu.make_async_remote_copy(
            src_ref=ext.at[src],
            dst_ref=ext.at[dst],
            send_sem=send_sem.at[n],
            recv_sem=recv_sem.at[n],
            device_id=partner(dy, dx),
            device_id_type=MESH,
        )
        sends.append((dy, dx, copy))
        where_inside(dy, copy.start)

    def arrived(dy, dx):
        for route_y, route_x, copy in sends:
            if (route_y, route_x) == (dy, dx):
                where_inside(-dy, copy.wait_recv)

    for i in range(2):
        jobs = [(j, p) for j in range(2) for p in range(PAIRS)]
        quads = [(slice(2 * i, 2 * i + 2), slice(2 * j, 2 * j + 2), slice(None)) for j in range(2)]
        rows = [slice(WIN * (2 * i + j), WIN * (2 * i + j) + WIN) for j in range(2)]
        cols = [slice(128 * p, 128 * p + 128) for p in range(PAIRS)]
        outs = attend(
            [q0[(*quads[j], cols[p])].reshape(WIN, 128) for j, p in jobs],
            [kv0[rows[j], cols[p]] for j, p in jobs],
            [kv0[rows[j], D + 128 * p:D + 128 * p + 128] for j, p in jobs],
            [bias0[p] for j, p in jobs],
        )
        for (j, p), o in zip(jobs, outs):
            ctx[(*quads[j], cols[p])] = o.reshape(2, 2, QUAD, 128)
        band = slice(2 * i, 2 * i + 2)
        update = jnp.dot(ctx[band].reshape(128, D), wproj[0], preferred_element_type=F32)
        cells = xq[band].reshape(128, D) + update
        xq[band] = cells.reshape(2, 4, QUAD, D)
        unit = layer_norm(cells, gain[1:2, :]).astype(BF16)
        ext[1 + 2 * i:3 + 2 * i, OWN] = unit.reshape(2, 4, QUAD, D)
        if i == 0:
            inner = (lat > 0) & (lat < n_lat - 1)
            pl.when(inner)(lambda: pl.semaphore_wait(barrier, 8))
            pl.when(jnp.logical_not(inner))(lambda: pl.semaphore_wait(barrier, 5))
        for n, route in enumerate(WAVES[i]):
            send(len(WAVES[0]) * i + n, *route)

    for copy in ld_qkv[1]:
        copy.wait()
    own = ext[OWN, OWN].reshape(256, D)
    own_q = jnp.dot(own, wqkv[1, :, :D], preferred_element_type=F32) * 0.125
    q1[...] = own_q.astype(BF16).reshape(4, 4, QUAD, D)
    own_kv = jnp.dot(own, wqkv[1, :, D:], preferred_element_type=F32)
    kv1[OWN, OWN] = own_kv.astype(BF16).reshape(4, 4, QUAD, 2 * D)
    ld_bias[1].wait()
    ld_proj[1].wait()
    row = lax.broadcasted_iota(jnp.int32, (128, 128), 0)
    lane = lax.broadcasted_iota(jnp.int32, (128, 128), 1)
    key_order = (natural_of_quad((128, 128), 1) + (lane & 64) == row).astype(F32)
    for p in range(PAIRS):
        b = jnp.dot(
            pair_bias(1, p), key_order, precision=lax.Precision.HIGHEST, preferred_element_type=F32
        )
        bias1[p] = b.reshape(2, 2, QUAD, 128)

    @pl.when(lat == 0)
    def _():
        ext[0] = jnp.zeros((6, QUAD, D), BF16)

    @pl.when(lat == n_lat - 1)
    def _():
        ext[5] = jnp.zeros((6, QUAD, D), BF16)

    north = (lax.broadcasted_iota(jnp.int32, (1, 128), 1) & 63) < 32
    closed = {
        0: jnp.where(north, jnp.where(lat == 0, -1e30, 0.0), 0.0),
        2: jnp.where(north, 0.0, jnp.where(lat == n_lat - 1, -1e30, 0.0)),
    }

    def shifted(group):
        qs, ks, vs, biases, places = [], [], [], [], []
        for a, b in group:
            r0, r1 = max(2 * a - 1, 0), min(2 * a, 3) + 1
            c0, c1 = max(2 * b - 1, 0), min(2 * b, 3) + 1
            u0, v0 = r0 - (2 * a - 1), c0 - (2 * b - 1)
            nr, nc = r1 - r0, c1 - c0
            count = nr * nc * QUAD
            here = (slice(2 * a, 2 * a + 2), slice(2 * b, 2 * b + 2), slice(None))
            for p in range(PAIRS):
                col = slice(128 * p, 128 * p + 128)
                place = (slice(r0, r1), slice(c0, c1), slice(None), col)
                part = bias1[p, u0:u0 + nr, v0:v0 + nc].reshape(count, 128)
                if a in closed:
                    part = part + closed[a]
                biases.append(part)
                qs.append(q1[place].reshape(count, 128))
                ks.append(kv1[(*here, col)].reshape(WIN, 128))
                vs.append(kv1[(*here, slice(D + 128 * p, D + 128 * p + 128))].reshape(WIN, 128))
                places.append((place, (nr, nc, QUAD, 128)))
        for (place, shape), o in zip(places, attend(qs, ks, vs, biases)):
            ctx[place] = o.reshape(shape)

    def halo_kv(units):
        return jnp.dot(units, wqkv[1, :, D:], preferred_element_type=F32).astype(BF16)

    stores = []

    def finish(bands):
        block = jnp.concatenate([ctx[r].reshape(WIN, D) for r in bands], axis=0)
        update = jnp.dot(block, wproj[1], preferred_element_type=F32)
        for n, r in enumerate(bands):
            cells = xq[r] + update[WIN * n:WIN * n + WIN].reshape(4, QUAD, D)
            for j in range(2):
                left, right = [cells[2 * j + v].reshape(2, 8, D) for v in range(2)]
                x[4 * r:4 * r + 4, 8 * j:8 * j + 8, :] = from_quads(left, right)
            rows = pl.ds(4 * r, 4)
            store = pltpu.make_async_copy(x.at[rows], out.at[rows], out_sem.at[r])
            store.start()
            stores.append(store)

    shifted([(1, 1)])
    arrived(0, -1)
    arrived(0, 1)
    units = jnp.concatenate([ext[OWN, 0].reshape(64, D), ext[OWN, 5].reshape(64, D)], axis=0)
    got = halo_kv(units)
    kv1[OWN, 0] = got[:64].reshape(4, QUAD, 2 * D)
    kv1[OWN, 5] = got[64:].reshape(4, QUAD, 2 * D)
    shifted([(1, 0), (1, 2)])
    finish([1, 2])
    for a, dy in ((2, -1), (0, 1)):
        for dx in (0, -1, 1):
            arrived(dy, dx)
        edge = 5 if a == 2 else 0
        kv1[edge] = halo_kv(ext[edge].reshape(96, D)).reshape(6, QUAD, 2 * D)
        shifted([(a, 0), (a, 1), (a, 2)])
    finish([0, 3])
    for dy, _, copy in sends:
        where_inside(dy, copy.wait_send)
    for store in stores:
        store.wait()


def on_device(field, w_qkv, w_proj, norm_gain, pos_bias):
    rows, cols, width = field.shape
    any_space = pl.BlockSpec(memory_space=pl.ANY)
    vmem = pltpu.VMEM
    return pl.pallas_call(
        kernel,
        out_shape=jax.ShapeDtypeStruct(field.shape, F32),
        in_specs=[any_space] * 5,
        out_specs=any_space,
        scratch_shapes=[
            vmem((rows, cols, D), F32),
            vmem((4, 4, QUAD, D), F32),
            vmem((2, D, 3 * D), BF16),
            vmem((2, D, D), BF16),
            vmem((2, D), F32),
            vmem((2, HEADS, WIN, WIN), F32),
            vmem((PAIRS, WIN, 128), F32),
            vmem((PAIRS, 2, 2, QUAD, 128), F32),
            vmem((256, D), BF16),
            vmem((4, 4, QUAD, D), BF16),
            vmem((4, 4, QUAD, D), BF16),
            vmem((256, 2 * D), BF16),
            vmem((6, 6, QUAD, D), BF16),
            vmem((4, 4, QUAD, D), BF16),
            vmem((6, 6, QUAD, 2 * D), BF16),
            vmem((4, 4, QUAD, D), BF16),
            pltpu.SemaphoreType.DMA((12,)),
            pltpu.SemaphoreType.DMA((4,)),
            pltpu.SemaphoreType.DMA((10,)),
            pltpu.SemaphoreType.DMA((10,)),
        ],
        compiler_params=pltpu.CompilerParams(
            collective_id=0, has_side_effects=True, vmem_limit_bytes=48 * 1024 * 1024
        ),
        cost_estimate=pl.CostEstimate(
            flops=3_300_000_000, bytes_accessed=13_000_000, transcendentals=400_000
        ),
        name="swin_pair",
    )(*[pltpu.with_memory_space_constraint(a, pltpu.HBM) for a in (field, w_qkv, w_proj, norm_gain, pos_bias)])


def solution(mesh):
    return jax.shard_map(
        on_device,
        mesh=mesh,
        in_specs=(P("lat", "lon", None), P(), P(), P(), P()),
        out_specs=P("lat", "lon", None),
        check_vma=False,
    )
```

time: 28.3 us -> 21.9 us (0.77)
  local copies, waits for them, and re-layouts: 5.5 us -> 0.88 us
  Pallas kernels: 22.6 us -> 20.9 us
    unnamed x9 -> x1, local copies, waits for them, and re-layouts: 5.5 us -> 0.88 us
    pallas_call x1, Pallas kernels: 22.6 us -> 20.9 us  [on_device(): pl.pallas_call(kernel, out_shape=jax.ShapeDtypeStruct(field.shape, F32),...]
where the time goes in v2:
time: 21.9 us; the launch traced here: 21.8 us
  Pallas kernels  20.9 us (95%)
  local copies, waits for them, and re-layouts  0.88 us (4%)
    pallas_call x1, Pallas kernels, on_device(): pl.pallas_call(kernel, out_shape=jax.ShapeDtypeStruct(field.shape, F32),...  20.9 us
    unnamed x1, local copies, waits for them, and re-layouts  0.88 us

profile of v2, /device:TPU:1, one launch (start us, length us, event | category | flops | bytes accessed | tf_op | source)
XLA Modules:
  0.0 21.8 jit_solution(2913407668905788950)
XLA Ops:
  0.0 20.9 %swin_pair.1 = f32[16,16,768]{2,1,0:T(8,128)S(1)} custom-call(f32[16,16,768]{2,1,0:T(8,128)} %field.1, bf16[2,768,2304]{2,1,0:T(8,128)(2,1)} %w_qkv.1, bf16[2,768,768]{2,1,0:T(8,128)(2,1)} %w_proj.1, f32[2,768]{1,0:T(2,128)} %gains.1, f32[2,12,64,64]{3,2,1,0:T(8,128)} %pos_bias.1), custom_call_target="tpu_custom_call" | custom-call | flops 3300000000 | bytes 13000000 | tf_op jit(solution)/shard_map/swin_pair/pallas_call | solution.py:327
  21.0 0.9 %copy.7 = f32[16,16,768]{2,1,0:T(8,128)} copy(f32[16,16,768]{2,1,0:T(8,128)S(1)} %swin_pair.1) | data formatting | bytes 1572864

commit v3 on v2

--- a/solution.py
+++ b/solution.py
@@ -19,25 +19,7 @@
 
 PEERS = ((-1, 0), (1, 0), (0, -1), (0, 1), (-1, -1), (-1, 1), (1, -1), (1, 1))
 OWN = slice(1, 5)
-
-
-def piece(dy, dx, rows=OWN):
-    def axis(step, run):
-        if step == 0:
-            return pl.ds(run.start, run.stop - run.start), pl.ds(run.start, run.stop - run.start)
-        return (pl.ds(1, 1), pl.ds(5, 1)) if step < 0 else (pl.ds(4, 1), pl.ds(0, 1))
-
-    (src_r, dst_r), (src_c, dst_c) = axis(dy, rows), axis(dx, OWN)
-    return dy, dx, (src_r, src_c), (dst_r, dst_c)
-
-
-WAVES = tuple(
-    (
-        piece(dy, 0), piece(dy, -1), piece(dy, 1),
-        piece(0, -1, slice(top, top + 2)), piece(0, 1, slice(top, top + 2)),
-    )
-    for dy, top in ((-1, 1), (1, 3))
-)
+WAVE = 5
 
 
 def layer_norm(x, gain):
@@ -119,15 +101,15 @@
     def partner(dy, dx):
         return {"lat": lax.rem(lat + dy + n_lat, n_lat), "lon": lax.rem(lon + dx + n_lon, n_lon)}
 
-    def where_inside(dy, act):
-        if dy == 0:
-            act()
-        else:
-            pl.when(lat > 0 if dy < 0 else lat < n_lat - 1)(act)
+    def inside(dy):
+        return (lat + dy >= 0) & (lat + dy < n_lat)
+
+    odd = lax.rem(lat, 2)
+    order = (odd, 1 - odd)
 
     barrier = pltpu.get_barrier_semaphore()
     for dy, dx in PEERS:
-        where_inside(dy, lambda: pl.semaphore_signal(
+        pl.when(inside(dy))(lambda: pl.semaphore_signal(
             barrier, inc=1, device_id=partner(dy, dx), device_id_type=MESH))
 
     loads = []
@@ -167,7 +149,7 @@
         part = jnp.dot(
             normed[...], wqkv[0, :, D + D * c:2 * D + D * c], preferred_element_type=F32
         )
-        kv0[:, D * c:D * c + D] = part.astype(BF16)
+        kv0[:, :, D * c:D * c + D] = part.astype(BF16).reshape(4, WIN, D)
     ld_bias[0].wait()
 
     def pair_bias(s, p):
@@ -176,13 +158,11 @@
 
     for p in range(PAIRS):
         bias0[p] = pair_bias(0, p)
-    ld_proj[0].wait()
-    for copy in [*ld_qkv[1], ld_bias[1], ld_proj[1]]:
-        copy.start()
-
-    sends = []
-
-    def send(n, dy, dx, src, dst):
+
+    waves = ([], [])
+
+    def send(wave, dy, dx, src, dst):
+        n = WAVE * wave + len(waves[wave])
         copy = pltpu.make_async_remote_copy(
             src_ref=ext.at[src],
             dst_ref=ext.at[dst],
@@ -191,39 +171,50 @@
             device_id=partner(dy, dx),
             device_id_type=MESH,
         )
-        sends.append((dy, dx, copy))
-        where_inside(dy, copy.start)
-
-    def arrived(dy, dx):
-        for route_y, route_x, copy in sends:
-            if (route_y, route_x) == (dy, dx):
-                where_inside(-dy, copy.wait_recv)
-
-    for i in range(2):
+        waves[wave].append(copy)
+        return copy
+
+    for wave, i in enumerate(order):
+        band = pl.ds(2 * i, 2)
         jobs = [(j, p) for j in range(2) for p in range(PAIRS)]
-        quads = [(slice(2 * i, 2 * i + 2), slice(2 * j, 2 * j + 2), slice(None)) for j in range(2)]
-        rows = [slice(WIN * (2 * i + j), WIN * (2 * i + j) + WIN) for j in range(2)]
+        quads = [(band, slice(2 * j, 2 * j + 2), slice(None)) for j in range(2)]
         cols = [slice(128 * p, 128 * p + 128) for p in range(PAIRS)]
         outs = attend(
             [q0[(*quads[j], cols[p])].reshape(WIN, 128) for j, p in jobs],
-            [kv0[rows[j], cols[p]] for j, p in jobs],
-            [kv0[rows[j], D + 128 * p:D + 128 * p + 128] for j, p in jobs],
+            [kv0[pl.ds(2 * i + j, 1), :, cols[p]].reshape(WIN, 128) for j, p in jobs],
+            [kv0[pl.ds(2 * i + j, 1), :, D + 128 * p:D + 128 * p + 128].reshape(WIN, 128) for j, p in jobs],
             [bias0[p] for j, p in jobs],
         )
         for (j, p), o in zip(jobs, outs):
             ctx[(*quads[j], cols[p])] = o.reshape(2, 2, QUAD, 128)
-        band = slice(2 * i, 2 * i + 2)
+        if wave == 0:
+            ld_proj[0].wait()
+            for copy in [*ld_qkv[1], ld_bias[1], ld_proj[1]]:
+                copy.start()
         update = jnp.dot(ctx[band].reshape(128, D), wproj[0], preferred_element_type=F32)
         cells = xq[band].reshape(128, D) + update
         xq[band] = cells.reshape(2, 4, QUAD, D)
         unit = layer_norm(cells, gain[1:2, :]).astype(BF16)
-        ext[1 + 2 * i:3 + 2 * i, OWN] = unit.reshape(2, 4, QUAD, D)
-        if i == 0:
+        ext[pl.ds(1 + 2 * i, 2), OWN] = unit.reshape(2, 4, QUAD, D)
+        if wave == 0:
             inner = (lat > 0) & (lat < n_lat - 1)
             pl.when(inner)(lambda: pl.semaphore_wait(barrier, 8))
             pl.when(jnp.logical_not(inner))(lambda: pl.semaphore_wait(barrier, 5))
-        for n, route in enumerate(WAVES[i]):
-            send(len(WAVES[0]) * i + n, *route)
+        half = pl.ds(1 + 2 * i, 2)
+        send(wave, 0, -1, (half, slice(1, 2)), (half, slice(5, 6))).start()
+        send(wave, 0, 1, (half, slice(4, 5)), (half, slice(0, 1))).start()
+        dy = 2 * i - 1
+        here, there = pl.ds(1 + 3 * i, 1), pl.ds(5 - 5 * i, 1)
+        outward = (
+            send(wave, dy, 0, (here, slice(1, 5)), (there, slice(1, 5))),
+            send(wave, dy, -1, (here, slice(1, 2)), (there, slice(5, 6))),
+            send(wave, dy, 1, (here, slice(4, 5)), (there, slice(0, 1))),
+        )
+
+        @pl.when(inside(dy))
+        def _():
+            for copy in outward:
+                copy.start()
 
     for copy in ld_qkv[1]:
         copy.wait()
@@ -252,33 +243,32 @@
         ext[5] = jnp.zeros((6, QUAD, D), BF16)
 
     north = (lax.broadcasted_iota(jnp.int32, (1, 128), 1) & 63) < 32
-    closed = {
-        0: jnp.where(north, jnp.where(lat == 0, -1e30, 0.0), 0.0),
-        2: jnp.where(north, 0.0, jnp.where(lat == n_lat - 1, -1e30, 0.0)),
-    }
 
     def shifted(group):
         qs, ks, vs, biases, places = [], [], [], [], []
-        for a, b in group:
-            r0, r1 = max(2 * a - 1, 0), min(2 * a, 3) + 1
+        for r0, nr, u0, k0, b, closed in group:
             c0, c1 = max(2 * b - 1, 0), min(2 * b, 3) + 1
-            u0, v0 = r0 - (2 * a - 1), c0 - (2 * b - 1)
-            nr, nc = r1 - r0, c1 - c0
+            v0, nc = c0 - (2 * b - 1), c1 - c0
             count = nr * nc * QUAD
-            here = (slice(2 * a, 2 * a + 2), slice(2 * b, 2 * b + 2), slice(None))
+            here = (pl.ds(k0, 2), slice(2 * b, 2 * b + 2), slice(None))
             for p in range(PAIRS):
                 col = slice(128 * p, 128 * p + 128)
-                place = (slice(r0, r1), slice(c0, c1), slice(None), col)
-                part = bias1[p, u0:u0 + nr, v0:v0 + nc].reshape(count, 128)
-                if a in closed:
-                    part = part + closed[a]
-                biases.append(part)
+                place = (pl.ds(r0, nr), slice(c0, c1), slice(None), col)
+                part = bias1[p:p + 1, pl.ds(u0, nr), v0:v0 + nc].reshape(count, 128)
+                biases.append(part if closed is None else part + closed)
                 qs.append(q1[place].reshape(count, 128))
                 ks.append(kv1[(*here, col)].reshape(WIN, 128))
                 vs.append(kv1[(*here, slice(D + 128 * p, D + 128 * p + 128))].reshape(WIN, 128))
                 places.append((place, (nr, nc, QUAD, 128)))
         for (place, shape), o in zip(places, attend(qs, ks, vs, biases)):
             ctx[place] = o.reshape(shape)
+
+    middle = [(1, 2, 0, 2, b, None) for b in range(3)]
+
+    def edge(i):
+        shut = jnp.where(inside(2 * i - 1), 0.0, -1e30)
+        closed = jnp.where(north, jnp.where(i == 0, shut, 0.0), jnp.where(i == 1, shut, 0.0))
+        return [(3 * i, 1, 1 - i, 4 * i, b, closed) for b in range(3)]
 
     def halo_kv(units):
         return jnp.dot(units, wqkv[1, :, D:], preferred_element_type=F32).astype(BF16)
@@ -298,24 +288,42 @@
             store.start()
             stores.append(store)
 
-    shifted([(1, 1)])
-    arrived(0, -1)
-    arrived(0, 1)
-    units = jnp.concatenate([ext[OWN, 0].reshape(64, D), ext[OWN, 5].reshape(64, D)], axis=0)
+    shifted([middle[1]])
+    for wave in range(2):
+        for copy in waves[wave][:2]:
+            copy.wait_recv()
+
+    def edge_arrived(wave):
+        @pl.when(inside(2 * order[wave] - 1))
+        def _():
+            for copy in waves[wave][2:]:
+                copy.wait_recv()
+
+    edge_arrived(0)
+    far = 5 * order[0]
+    units = jnp.concatenate(
+        [ext[OWN, 0].reshape(64, D), ext[OWN, 5].reshape(64, D), ext[far].reshape(96, D)], axis=0
+    )
     got = halo_kv(units)
     kv1[OWN, 0] = got[:64].reshape(4, QUAD, 2 * D)
-    kv1[OWN, 5] = got[64:].reshape(4, QUAD, 2 * D)
-    shifted([(1, 0), (1, 2)])
+    kv1[OWN, 5] = got[64:128].reshape(4, QUAD, 2 * D)
+    kv1[far] = got[128:].reshape(6, QUAD, 2 * D)
+    shifted([middle[0], middle[2], *edge(order[0])])
     finish([1, 2])
-    for a, dy in ((2, -1), (0, 1)):
-        for dx in (0, -1, 1):
-            arrived(dy, dx)
-        edge = 5 if a == 2 else 0
-        kv1[edge] = halo_kv(ext[edge].reshape(96, D)).reshape(6, QUAD, 2 * D)
-        shifted([(a, 0), (a, 1), (a, 2)])
+    edge_arrived(1)
+    far = 5 * order[1]
+    kv1[far] = halo_kv(ext[far].reshape(96, D)).reshape(6, QUAD, 2 * D)
+    shifted(edge(order[1]))
     finish([0, 3])
-    for dy, _, copy in sends:
-        where_inside(dy, copy.wait_send)
+    for wave in range(2):
+        for copy in waves[wave][:2]:
+            copy.wait_send()
+
+        @pl.when(inside(2 * order[wave] - 1))
+        def _():
+            for copy in waves[wave][2:]:
+                copy.wait_send()
+
     for store in stores:
         store.wait()
 
@@ -341,15 +349,15 @@
             vmem((256, D), BF16),
             vmem((4, 4, QUAD, D), BF16),
             vmem((4, 4, QUAD, D), BF16),
-            vmem((256, 2 * D), BF16),
+            vmem((4, WIN, 2 * D), BF16),
             vmem((6, 6, QUAD, D), BF16),
             vmem((4, 4, QUAD, D), BF16),
             vmem((6, 6, QUAD, 2 * D), BF16),
             vmem((4, 4, QUAD, D), BF16),
             pltpu.SemaphoreType.DMA((12,)),
             pltpu.SemaphoreType.DMA((4,)),
-            pltpu.SemaphoreType.DMA((10,)),
-            pltpu.SemaphoreType.DMA((10,)),
+            pltpu.SemaphoreType.DMA((2 * WAVE,)),
+            pltpu.SemaphoreType.DMA((2 * WAVE,)),
         ],
         compiler_params=pltpu.CompilerParams(
             collective_id=0, has_side_effects=True, vmem_limit_bytes=48 * 1024 * 1024

time: 21.9 us -> 19.8 us (0.904)
  Pallas kernels: 20.9 us -> 18.9 us
    pallas_call x1, Pallas kernels: 20.9 us -> 18.9 us  [on_device(): pl.pallas_call(kernel, out_shape=jax.ShapeDtypeStruct(field.shape, F32),...]
where the time goes in v3:
time: 19.8 us
  Pallas kernels  18.9 us (95%)
  local copies, waits for them, and re-layouts  0.88 us (4%)
    pallas_call x1, Pallas kernels, on_device(): pl.pallas_call(kernel, out_shape=jax.ShapeDtypeStruct(field.shape, F32),...  18.9 us
    unnamed x1, local copies, waits for them, and re-layouts  0.88 us

profile of v3, /device:TPU:1, one launch (start us, length us, event | category | flops | bytes accessed | tf_op | source)
XLA Modules:
  0.0 19.8 jit_solution(890471122962173661)
XLA Ops:
  0.0 18.9 %swin_pair.1 = f32[16,16,768]{2,1,0:T(8,128)S(1)} custom-call(f32[16,16,768]{2,1,0:T(8,128)} %field.1, bf16[2,768,2304]{2,1,0:T(8,128)(2,1)} %w_qkv.1, bf16[2,768,768]{2,1,0:T(8,128)(2,1)} %w_proj.1, f32[2,768]{1,0:T(2,128)} %gains.1, f32[2,12,64,64]{3,2,1,0:T(8,128)} %pos_bias.1), custom_call_target="tpu_custom_call" | custom-call | flops 3300000000 | bytes 13000000 | tf_op jit(solution)/shard_map/swin_pair/pallas_call | solution.py:335
  18.9 0.9 %copy.7 = f32[16,16,768]{2,1,0:T(8,128)} copy(f32[16,16,768]{2,1,0:T(8,128)S(1)} %swin_pair.1) | data formatting | bytes 1572864

commit v4 on v3

--- a/solution.py
+++ b/solution.py
@@ -273,7 +273,6 @@
     def halo_kv(units):
         return jnp.dot(units, wqkv[1, :, D:], preferred_element_type=F32).astype(BF16)
 
-    stores = []
 
     def finish(bands):
         block = jnp.concatenate([ctx[r].reshape(WIN, D) for r in bands], axis=0)
@@ -282,11 +281,7 @@
             cells = xq[r] + update[WIN * n:WIN * n + WIN].reshape(4, QUAD, D)
             for j in range(2):
                 left, right = [cells[2 * j + v].reshape(2, 8, D) for v in range(2)]
-                x[4 * r:4 * r + 4, 8 * j:8 * j + 8, :] = from_quads(left, right)
-            rows = pl.ds(4 * r, 4)
-            store = pltpu.make_async_copy(x.at[rows], out.at[rows], out_sem.at[r])
-            store.start()
-            stores.append(store)
+                out[4 * r:4 * r + 4, 8 * j:8 * j + 8, :] = from_quads(left, right)
 
     shifted([middle[1]])
     for wave in range(2):
@@ -324,9 +319,6 @@
             for copy in waves[wave][2:]:
                 copy.wait_send()
 
-    for store in stores:
-        store.wait()
-
 
 def on_device(field, w_qkv, w_proj, norm_gain, pos_bias):
     rows, cols, width = field.shape
@@ -336,7 +328,7 @@
         kernel,
         out_shape=jax.ShapeDtypeStruct(field.shape, F32),
         in_specs=[any_space] * 5,
-        out_specs=any_space,
+        out_specs=pl.BlockSpec(memory_space=pltpu.VMEM),
         scratch_shapes=[
             vmem((rows, cols, D), F32),
             vmem((4, 4, QUAD, D), F32),

time: 19.8 us -> 18.6 us (0.939)
  Pallas kernels: 18.9 us -> 17.6 us
    pallas_call x1, Pallas kernels: 18.9 us -> 17.6 us  [on_device(): pl.pallas_call(kernel, out_shape=jax.ShapeDtypeStruct(field.shape, F32),...]
where the time goes in v4:
time: 18.6 us; the launch traced here: 18.5 us
  Pallas kernels  17.6 us (95%)
  local copies, waits for them, and re-layouts  0.88 us (5%)
    pallas_call x1, Pallas kernels, on_device(): pl.pallas_call(kernel, out_shape=jax.ShapeDtypeStruct(field.shape, F32),...  17.6 us
    unnamed x1, local copies, waits for them, and re-layouts  0.88 us

profile of v4, /device:TPU:1, one launch (start us, length us, event | category | flops | bytes accessed | tf_op | source)
XLA Modules:
  0.0 18.5 jit_solution(4465500012397447526)
XLA Ops:
  0.0 17.6 %swin_pair.1 = f32[16,16,768]{2,1,0:T(8,128)S(1)} custom-call(f32[16,16,768]{2,1,0:T(8,128)} %field.1, bf16[2,768,2304]{2,1,0:T(8,128)(2,1)} %w_qkv.1, bf16[2,768,768]{2,1,0:T(8,128)(2,1)} %w_proj.1, f32[2,768]{1,0:T(2,128)} %gains.1, f32[2,12,64,64]{3,2,1,0:T(8,128)} %pos_bias.1), custom_call_target="tpu_custom_call" | custom-call | flops 3300000000 | bytes 13000000 | tf_op jit(solution)/shard_map/swin_pair/pallas_call | solution.py:327
  17.6 0.9 %copy.7 = f32[16,16,768]{2,1,0:T(8,128)} copy(f32[16,16,768]{2,1,0:T(8,128)S(1)} %swin_pair.1) | data formatting | bytes 1572864

commit v5 on v4

--- a/solution.py
+++ b/solution.py
@@ -17,9 +17,8 @@
 MESH = pl.DeviceIdType.MESH
 NT = (((1,), (1,)), ((), ()))
 
-PEERS = ((-1, 0), (1, 0), (0, -1), (0, 1), (-1, -1), (-1, 1), (1, -1), (1, 1))
 OWN = slice(1, 5)
-WAVE = 5
+WAVE = 6
 
 
 def layer_norm(x, gain):
@@ -107,8 +106,11 @@
     odd = lax.rem(lat, 2)
     order = (odd, 1 - odd)
 
+    core = lax.rem(lon, 2)
+    outside = 2 * core - 1
+
     barrier = pltpu.get_barrier_semaphore()
-    for dy, dx in PEERS:
+    for dy, dx in ((0, -1), (0, 1), (-1, 0), (1, 0), (-1, outside), (1, outside)):
         pl.when(inside(dy))(lambda: pl.semaphore_signal(
             barrier, inc=1, device_id=partner(dy, dx), device_id_type=MESH))
 
@@ -138,18 +140,15 @@
             quads = (slice(2 * i, 2 * i + 2), slice(2 * j, 2 * j + 2))
             cells = x[8 * i:8 * i + 8, 8 * j:8 * j + 8, :]
             unit = layer_norm(cells, gain[0:1, :])
-            normed[WIN * w:WIN * w + WIN, :] = unit.reshape(WIN, D).astype(BF16)
+            normed[w] = unit.reshape(WIN, D).astype(BF16)
             nquad[quads] = window_quads(unit).astype(BF16)
             xq[quads] = window_quads(cells)
     ld_qkv[0][0].wait()
     part = jnp.dot(nquad[...].reshape(256, D), wqkv[0, :, :D], preferred_element_type=F32) * 0.125
     q0[...] = part.astype(BF16).reshape(4, 4, QUAD, D)
-    for c in range(2):
-        ld_qkv[0][1 + c].wait()
-        part = jnp.dot(
-            normed[...], wqkv[0, :, D + D * c:2 * D + D * c], preferred_element_type=F32
-        )
-        kv0[:, :, D * c:D * c + D] = part.astype(BF16).reshape(4, WIN, D)
+    ld_qkv[0][1].wait()
+    part = jnp.dot(normed[...].reshape(256, D), wqkv[0, :, D:2 * D], preferred_element_type=F32)
+    kv0[:, :, :D] = part.astype(BF16).reshape(4, WIN, D)
     ld_bias[0].wait()
 
     def pair_bias(s, p):
@@ -176,6 +175,13 @@
 
     for wave, i in enumerate(order):
         band = pl.ds(2 * i, 2)
+        pair = pl.ds(2 * i, 2)
+        if wave == 0:
+            ld_qkv[0][2].wait()
+        part = jnp.dot(
+            normed[pair].reshape(128, D), wqkv[0, :, 2 * D:], preferred_element_type=F32
+        )
+        kv0[pair, :, D:] = part.astype(BF16).reshape(2, WIN, D)
         jobs = [(j, p) for j in range(2) for p in range(PAIRS)]
         quads = [(band, slice(2 * j, 2 * j + 2), slice(None)) for j in range(2)]
         cols = [slice(128 * p, 128 * p + 128) for p in range(PAIRS)]
@@ -198,18 +204,24 @@
         ext[pl.ds(1 + 2 * i, 2), OWN] = unit.reshape(2, 4, QUAD, D)
         if wave == 0:
             inner = (lat > 0) & (lat < n_lat - 1)
-            pl.when(inner)(lambda: pl.semaphore_wait(barrier, 8))
-            pl.when(jnp.logical_not(inner))(lambda: pl.semaphore_wait(barrier, 5))
+            pl.when(inner)(lambda: pl.semaphore_wait(barrier, 6))
+            pl.when(jnp.logical_not(inner))(lambda: pl.semaphore_wait(barrier, 4))
         half = pl.ds(1 + 2 * i, 2)
-        send(wave, 0, -1, (half, slice(1, 2)), (half, slice(5, 6))).start()
-        send(wave, 0, 1, (half, slice(4, 5)), (half, slice(0, 1))).start()
         dy = 2 * i - 1
         here, there = pl.ds(1 + 3 * i, 1), pl.ds(5 - 5 * i, 1)
+        shared, rest = pl.ds(4 - 3 * core, 1), pl.ds(1 + core, 3)
+        west = send(wave, 0, -1, (half, slice(1, 2)), (half, slice(5, 6)))
+        east = send(wave, 0, 1, (half, slice(4, 5)), (half, slice(0, 1)))
+        first = send(wave, dy, 0, (here, shared), (there, shared))
         outward = (
-            send(wave, dy, 0, (here, slice(1, 5)), (there, slice(1, 5))),
-            send(wave, dy, -1, (here, slice(1, 2)), (there, slice(5, 6))),
-            send(wave, dy, 1, (here, slice(4, 5)), (there, slice(0, 1))),
+            send(wave, dy, 0, (here, rest), (there, rest)),
+            send(wave, dy, outside, (here, pl.ds(1 + 3 * core, 1)), (there, pl.ds(5 - 5 * core, 1))),
         )
+        far = pl.ds(5 * i, 1)
+        send(wave, 0, -outside, (far, shared), (far, pl.ds(5 * core, 1)))
+        pl.when(inside(dy))(first.start)
+        west.start()
+        east.start()
 
         @pl.when(inside(dy))
         def _():
@@ -275,41 +287,59 @@
 
 
     def finish(bands):
-        block = jnp.concatenate([ctx[r].reshape(WIN, D) for r in bands], axis=0)
+        block = jnp.concatenate([ctx[pl.ds(r, 1)].reshape(WIN, D) for r in bands], axis=0)
         update = jnp.dot(block, wproj[1], preferred_element_type=F32)
         for n, r in enumerate(bands):
-            cells = xq[r] + update[WIN * n:WIN * n + WIN].reshape(4, QUAD, D)
+            cells = xq[pl.ds(r, 1)].reshape(4, QUAD, D)
+            cells = cells + update[WIN * n:WIN * n + WIN].reshape(4, QUAD, D)
             for j in range(2):
                 left, right = [cells[2 * j + v].reshape(2, 8, D) for v in range(2)]
-                out[4 * r:4 * r + 4, 8 * j:8 * j + 8, :] = from_quads(left, right)
-
+                out[pl.ds(4 * r, 4), 8 * j:8 * j + 8, :] = from_quads(left, right)
+
+    def pass_on(wave):
+        @pl.when(inside(2 * order[wave] - 1))
+        def _():
+            waves[wave][2].wait_recv()
+            waves[wave][5].start()
+
+    pass_on(0)
     shifted([middle[1]])
-    for wave in range(2):
+    pass_on(1)
+    def sides_arrived(wave):
         for copy in waves[wave][:2]:
             copy.wait_recv()
 
     def edge_arrived(wave):
         @pl.when(inside(2 * order[wave] - 1))
         def _():
-            for copy in waves[wave][2:]:
+            for copy in waves[wave][3:]:
                 copy.wait_recv()
 
+    def side_units(wave):
+        half = pl.ds(1 + 2 * order[wave], 2)
+        return [ext[half, c:c + 1].reshape(32, D) for c in (0, 5)]
+
+    def side_kv(wave, got):
+        half = pl.ds(1 + 2 * order[wave], 2)
+        for n, c in enumerate((0, 5)):
+            kv1[half, c:c + 1] = got[32 * n:32 * n + 32].reshape(2, 1, QUAD, 2 * D)
+
+    sides_arrived(0)
     edge_arrived(0)
     far = 5 * order[0]
-    units = jnp.concatenate(
-        [ext[OWN, 0].reshape(64, D), ext[OWN, 5].reshape(64, D), ext[far].reshape(96, D)], axis=0
-    )
-    got = halo_kv(units)
-    kv1[OWN, 0] = got[:64].reshape(4, QUAD, 2 * D)
-    kv1[OWN, 5] = got[64:128].reshape(4, QUAD, 2 * D)
-    kv1[far] = got[128:].reshape(6, QUAD, 2 * D)
-    shifted([middle[0], middle[2], *edge(order[0])])
-    finish([1, 2])
+    got = halo_kv(jnp.concatenate([*side_units(0), ext[far].reshape(96, D)], axis=0))
+    side_kv(0, got)
+    kv1[far] = got[64:].reshape(6, QUAD, 2 * D)
+    shifted(edge(order[0]))
+    sides_arrived(1)
+    side_kv(1, halo_kv(jnp.concatenate(side_units(1), axis=0)))
+    shifted([middle[0], middle[2]])
+    finish([1, 2, 3 * order[0]])
     edge_arrived(1)
     far = 5 * order[1]
     kv1[far] = halo_kv(ext[far].reshape(96, D)).reshape(6, QUAD, 2 * D)
     shifted(edge(order[1]))
-    finish([0, 3])
+    finish([3 * order[1]])
     for wave in range(2):
         for copy in waves[wave][:2]:
             copy.wait_send()
@@ -338,7 +368,7 @@
             vmem((2, HEADS, WIN, WIN), F32),
             vmem((PAIRS, WIN, 128), F32),
             vmem((PAIRS, 2, 2, QUAD, 128), F32),
-            vmem((256, D), BF16),
+            vmem((4, WIN, D), BF16),
             vmem((4, 4, QUAD, D), BF16),
             vmem((4, 4, QUAD, D), BF16),
             vmem((4, WIN, 2 * D), BF16),

time: 18.6 us -> 18.1 us (0.973); the launches traced: 18.5 us -> 17.8 us
  Pallas kernels: 17.6 us -> 16.9 us
    pallas_call x1, Pallas kernels: 17.6 us -> 16.9 us  [on_device(): pl.pallas_call(kernel, out_shape=jax.ShapeDtypeStruct(field.shape, F32),...]
where the time goes in v5:
time: 18.1 us; the launch traced here: 17.8 us
  Pallas kernels  16.9 us (93%)
  local copies, waits for them, and re-layouts  0.88 us (5%)
    pallas_call x1, Pallas kernels, on_device(): pl.pallas_call(kernel, out_shape=jax.ShapeDtypeStruct(field.shape, F32),...  16.9 us
    unnamed x1, local copies, waits for them, and re-layouts  0.88 us

profile of v5, /device:TPU:1, one launch (start us, length us, event | category | flops | bytes accessed | tf_op | source)
XLA Modules:
  0.0 17.8 jit_solution(1366374749481377361)
XLA Ops:
  0.0 16.9 %swin_pair.1 = f32[16,16,768]{2,1,0:T(8,128)S(1)} custom-call(f32[16,16,768]{2,1,0:T(8,128)} %field.1, bf16[2,768,2304]{2,1,0:T(8,128)(2,1)} %w_qkv.1, bf16[2,768,768]{2,1,0:T(8,128)(2,1)} %w_proj.1, f32[2,768]{1,0:T(2,128)} %gains.1, f32[2,12,64,64]{3,2,1,0:T(8,128)} %pos_bias.1), custom_call_target="tpu_custom_call" | custom-call | flops 3300000000 | bytes 13000000 | tf_op jit(solution)/shard_map/swin_pair/pallas_call | solution.py:357
  16.9 0.9 %copy.7 = f32[16,16,768]{2,1,0:T(8,128)} copy(f32[16,16,768]{2,1,0:T(8,128)S(1)} %swin_pair.1) | data formatting | bytes 1572864

commit v6 on v5

--- a/solution.py
+++ b/solution.py
@@ -219,14 +219,14 @@
         )
         far = pl.ds(5 * i, 1)
         send(wave, 0, -outside, (far, shared), (far, pl.ds(5 * core, 1)))
-        pl.when(inside(dy))(first.start)
+        @pl.when(inside(dy))
+        def _():
+            first.start()
+            outward[1].start()
+
         west.start()
         east.start()
-
-        @pl.when(inside(dy))
-        def _():
-            for copy in outward:
-                copy.start()
+        pl.when(inside(dy))(outward[0].start)
 
     for copy in ld_qkv[1]:
         copy.wait()
@@ -304,7 +304,7 @@
 
     pass_on(0)
     shifted([middle[1]])
-    pass_on(1)
+
     def sides_arrived(wave):
         for copy in waves[wave][:2]:
             copy.wait_recv()
@@ -331,6 +331,7 @@
     side_kv(0, got)
     kv1[far] = got[64:].reshape(6, QUAD, 2 * D)
     shifted(edge(order[0]))
+    pass_on(1)
     sides_arrived(1)
     side_kv(1, halo_kv(jnp.concatenate(side_units(1), axis=0)))
     shifted([middle[0], middle[2]])

time: 18.1 us -> 18 us (level); the launches traced: 17.8 us -> 17.9 us
  no operation moved by 1% of the time
where the time goes in v6:
time: 18 us; the launch traced here: 17.9 us
  Pallas kernels  17 us (94%)
  local copies, waits for them, and re-layouts  0.88 us (5%)
    pallas_call x1, Pallas kernels, on_device(): pl.pallas_call(kernel, out_shape=jax.ShapeDtypeStruct(field.shape, F32),...  17 us
    unnamed x1, local copies, waits for them, and re-layouts  0.88 us

profile of v6, /device:TPU:1, one launch (start us, length us, event | category | flops | bytes accessed | tf_op | source)
XLA Modules:
  0.0 17.9 jit_solution(2529891282131099249)
XLA Ops:
  0.0 17.0 %swin_pair.1 = f32[16,16,768]{2,1,0:T(8,128)S(1)} custom-call(f32[16,16,768]{2,1,0:T(8,128)} %field.1, bf16[2,768,2304]{2,1,0:T(8,128)(2,1)} %w_qkv.1, bf16[2,768,768]{2,1,0:T(8,128)(2,1)} %w_proj.1, f32[2,768]{1,0:T(2,128)} %gains.1, f32[2,12,64,64]{3,2,1,0:T(8,128)} %pos_bias.1), custom_call_target="tpu_custom_call" | custom-call | flops 3300000000 | bytes 13000000 | tf_op jit(solution)/shard_map/swin_pair/pallas_call | solution.py:358
  17.0 0.9 %copy.7 = f32[16,16,768]{2,1,0:T(8,128)} copy(f32[16,16,768]{2,1,0:T(8,128)S(1)} %swin_pair.1) | data formatting | bytes 1572864

commit v7 on v6

--- a/solution.py
+++ b/solution.py
@@ -178,6 +178,8 @@
         pair = pl.ds(2 * i, 2)
         if wave == 0:
             ld_qkv[0][2].wait()
+            for copy in [*ld_qkv[1], ld_bias[1], ld_proj[1]]:
+                copy.start()
         part = jnp.dot(
             normed[pair].reshape(128, D), wqkv[0, :, 2 * D:], preferred_element_type=F32
         )
@@ -195,8 +197,6 @@
             ctx[(*quads[j], cols[p])] = o.reshape(2, 2, QUAD, 128)
         if wave == 0:
             ld_proj[0].wait()
-            for copy in [*ld_qkv[1], ld_bias[1], ld_proj[1]]:
-                copy.start()
         update = jnp.dot(ctx[band].reshape(128, D), wproj[0], preferred_element_type=F32)
         cells = xq[band].reshape(128, D) + update
         xq[band] = cells.reshape(2, 4, QUAD, D)
@@ -335,12 +335,12 @@
     sides_arrived(1)
     side_kv(1, halo_kv(jnp.concatenate(side_units(1), axis=0)))
     shifted([middle[0], middle[2]])
-    finish([1, 2, 3 * order[0]])
+    finish([1, 2])
     edge_arrived(1)
     far = 5 * order[1]
     kv1[far] = halo_kv(ext[far].reshape(96, D)).reshape(6, QUAD, 2 * D)
     shifted(edge(order[1]))
-    finish([3 * order[1]])
+    finish([0, 3])
     for wave in range(2):
         for copy in waves[wave][:2]:
             copy.wait_send()

time: 18 us -> 17.9 us (level)
  no operation moved by 1% of the time
where the time goes in v7:
time: 17.9 us; the launch traced here: 17.8 us
  Pallas kernels  16.9 us (94%)
  local copies, waits for them, and re-layouts  0.88 us (5%)
    pallas_call x1, Pallas kernels, on_device(): pl.pallas_call(kernel, out_shape=jax.ShapeDtypeStruct(field.shape, F32),...  16.9 us
    unnamed x1, local copies, waits for them, and re-layouts  0.88 us

profile of v7, /device:TPU:1, one launch (start us, length us, event | category | flops | bytes accessed | tf_op | source)
XLA Modules:
  0.0 17.8 jit_solution(17931202741298674187)
XLA Ops:
  0.0 16.9 %swin_pair.1 = f32[16,16,768]{2,1,0:T(8,128)S(1)} custom-call(f32[16,16,768]{2,1,0:T(8,128)} %field.1, bf16[2,768,2304]{2,1,0:T(8,128)(2,1)} %w_qkv.1, bf16[2,768,768]{2,1,0:T(8,128)(2,1)} %w_proj.1, f32[2,768]{1,0:T(2,128)} %gains.1, f32[2,12,64,64]{3,2,1,0:T(8,128)} %pos_bias.1), custom_call_target="tpu_custom_call" | custom-call | flops 3300000000 | bytes 13000000 | tf_op jit(solution)/shard_map/swin_pair/pallas_call | solution.py:358
  16.9 0.9 %copy.7 = f32[16,16,768]{2,1,0:T(8,128)} copy(f32[16,16,768]{2,1,0:T(8,128)S(1)} %swin_pair.1) | data formatting | bytes 1572864

commit v8 on v6

--- a/solution.py
+++ b/solution.py
@@ -109,11 +109,6 @@
     core = lax.rem(lon, 2)
     outside = 2 * core - 1
 
-    barrier = pltpu.get_barrier_semaphore()
-    for dy, dx in ((0, -1), (0, 1), (-1, 0), (1, 0), (-1, outside), (1, outside)):
-        pl.when(inside(dy))(lambda: pl.semaphore_signal(
-            barrier, inc=1, device_id=partner(dy, dx), device_id_type=MESH))
-
     loads = []
 
     def load(src, dst):
@@ -121,7 +116,7 @@
         loads.append(copy)
         return copy
 
-    ld_x = load(field, x)
+    ld_x = [load(field.at[pl.ds(8 * i, 8)], x.at[pl.ds(8 * i, 8)]) for i in range(2)]
     ld_gain = load(gains, gain)
     ld_qkv = [
         [load(w_qkv.at[s, :, pl.ds(D * c, D)], wqkv.at[s, :, pl.ds(D * c, D)]) for c in range(3)]
@@ -129,12 +124,17 @@
     ]
     ld_bias = [load(pos_bias.at[s], bias.at[s]) for s in range(2)]
     ld_proj = [load(w_proj.at[s], wproj.at[s]) for s in range(2)]
-    for copy in [ld_x, ld_gain, *ld_qkv[0], ld_bias[0], ld_proj[0]]:
+    for copy in [ld_x[0], ld_gain, ld_x[1], *ld_qkv[0], ld_bias[0], ld_proj[0]]:
         copy.start()
 
-    ld_x.wait()
+    barrier = pltpu.get_barrier_semaphore()
+    for dy, dx in ((0, -1), (0, 1), (-1, 0), (1, 0), (-1, outside), (1, outside)):
+        pl.when(inside(dy))(lambda: pl.semaphore_signal(
+            barrier, inc=1, device_id=partner(dy, dx), device_id_type=MESH))
+
     ld_gain.wait()
     for i in range(2):
+        ld_x[i].wait()
         for j in range(2):
             w = 2 * i + j
             quads = (slice(2 * i, 2 * i + 2), slice(2 * j, 2 * j + 2))
@@ -377,7 +377,7 @@
             vmem((4, 4, QUAD, D), BF16),
             vmem((6, 6, QUAD, 2 * D), BF16),
             vmem((4, 4, QUAD, D), BF16),
-            pltpu.SemaphoreType.DMA((12,)),
+            pltpu.SemaphoreType.DMA((13,)),
             pltpu.SemaphoreType.DMA((4,)),
             pltpu.SemaphoreType.DMA((2 * WAVE,)),
             pltpu.SemaphoreType.DMA((2 * WAVE,)),

time: 18 us -> 17.9 us (level)
  no operation moved by 1% of the time
where the time goes in v8:
time: 17.9 us
  Pallas kernels  17 us (95%)
  local copies, waits for them, and re-layouts  0.88 us (5%)
    pallas_call x1, Pallas kernels, on_device(): pl.pallas_call(kernel, out_shape=jax.ShapeDtypeStruct(field.shape, F32),...  17 us
    unnamed x1, local copies, waits for them, and re-layouts  0.88 us

profile of v8, /device:TPU:1, one launch (start us, length us, event | category | flops | bytes accessed | tf_op | source)
XLA Modules:
  0.0 17.9 jit_solution(14785077347460184449)
XLA Ops:
  0.0 17.0 %swin_pair.1 = f32[16,16,768]{2,1,0:T(8,128)S(1)} custom-call(f32[16,16,768]{2,1,0:T(8,128)} %field.1, bf16[2,768,2304]{2,1,0:T(8,128)(2,1)} %w_qkv.1, bf16[2,768,768]{2,1,0:T(8,128)(2,1)} %w_proj.1, f32[2,768]{1,0:T(2,128)} %gains.1, f32[2,12,64,64]{3,2,1,0:T(8,128)} %pos_bias.1), custom_call_target="tpu_custom_call" | custom-call | flops 3300000000 | bytes 13000000 | tf_op jit(solution)/shard_map/swin_pair/pallas_call | solution.py:358
  17.0 0.9 %copy.7 = f32[16,16,768]{2,1,0:T(8,128)} copy(f32[16,16,768]{2,1,0:T(8,128)S(1)} %swin_pair.1) | data formatting | bytes 1572864
